TPU v7x, 32 devices: a whole 2x2x4 slice. The times are simulated.
32 devices in a mesh: dp: 4 (over z), expert: 8 (over y, x, core).
Axes of the slice: x: 2, y: 2, z: 4, core: 2. Of those that a mesh axis runs over, the one named last changes fastest.
Arguments:
- inputs: bfloat16 [4, 3072, 768], P('dp', 'expert'), may hold values from -6 to 6
- gain_one: float32 [768], replicated, may hold values from 0.5 to 1.5
- w_query: bfloat16 [768, 768], replicated, may hold values from -0.21875 to 0.21875
- w_key: bfloat16 [768, 768], replicated, may hold values from -0.21875 to 0.21875
- w_value: bfloat16 [768, 768], replicated, may hold values from -0.21875 to 0.21875
- w_out_proj: bfloat16 [768, 768], replicated, may hold values from -1.25 to 1.25
- gain_two: float32 [768], replicated, may hold values from 0.5 to 1.5
- w_router: bfloat16 [768, 16], replicated, may hold values from -0.14941406 to 0.14941406
- w_in: bfloat16 [16, 768, 3072], P('expert'), may hold values from -0.21875 to 0.21875
- w_out: bfloat16 [16, 3072, 768], P('expert'), may hold values from -0.109375 to 0.109375
- routes: int32 [4, 3072, 2], P('dp', 'expert'), may hold values from 0 to 15, as said below
- slot_index: int32 [4, 3072, 2], P('dp', 'expert'), may hold values from 0 to 60, as said below
- prompt_of: int32 [4, 8], P('dp', 'expert'), may hold values from 0 to 1
- cotangent: bfloat16 [4, 3072, 768], P('dp', 'expert'), may hold values from -6 to 6
Outputs:
- outputs: bfloat16 [4, 3072, 768], P('dp', 'expert')
- grad_input: float32 [4, 3072, 768], P('dp', 'expert')
- grad_gain_one: float32 [768], replicated
- grad_query: float32 [768, 768], replicated
- grad_key: float32 [768, 768], replicated
- grad_value: float32 [768, 768], replicated
- grad_out_proj: float32 [768, 768], replicated
- grad_gain_two: float32 [768], replicated
- grad_router: float32 [768, 16], replicated
- grad_w_in: float32 [16, 768, 3072], P('expert', 'dp')
- grad_w_out: float32 [16, 3072, 768], P('expert', 'dp')
Inputs may be any that keep to these rules, and one draw needn't show every extreme that they name: `routes`: the two experts of a row differ. slot_index[g, t, k] counts the pairs before (t, k) in the rows of the same device (384 rows in a row, pairs in order of row, then k) that name the same expert, or is 60 where that count is 60 or more; such a pair is dropped.
All inputs are finite; a program needn't handle non-finite values.
Results may differ from a plain program's by a relative error of at most 0.015.
Values may be sent and summed in bfloat16 or wider, within the bound.
No kernel may reach another device: no remote copies, remote signals or barrier semaphores. Data moves between devices by JAX's collectives and lax.ppermute only.
A program may use at most 256 MiB of HBM per device.

v0:
```python
import jax
import jax.numpy as jnp
from jax import lax
from jax.sharding import PartitionSpec as P

H = 12
HD = 64
TOP = 2
NPR = 2
CLEN = 128
PR_DEV = 128


NEGATIVE = -1e30


def normed(values):
    return values * lax.rsqrt(jnp.mean(values * values, axis=-1, keepdims=True) + 1e-06)


def norm_back(values, grad):
    return jax.vjp(normed, values)[1](grad)[0]


def gelu_back(values, grad):
    return jax.vjp(jax.nn.gelu, values)[1](grad)[0]


def stats_update(running, affinity_table, visible):
    old_max, old_total = running
    new_max = jnp.maximum(old_max, jnp.max(jnp.where(visible, affinity_table, NEGATIVE), axis=-1))
    fresh = jnp.where(visible, jnp.exp(affinity_table - new_max[..., None]), 0.0)
    return (new_max, old_total * jnp.exp(old_max - new_max) + jnp.sum(fresh, axis=-1))


def likely(affinity_table, visible, log_total):
    return jnp.where(visible, jnp.exp(affinity_table - log_total[..., None]), 0.0)


def prompt_scores(queries, block_keys, query_pos, key_pos, score_scale):
    affinity_table = (
        jnp.einsum("qbhd,kbhd->bhqk", queries, block_keys, preferred_element_type=jnp.float32)
        * score_scale
    )
    return (affinity_table, key_pos[None, None, None, :] <= query_pos[None, None, :, None])


def cont_scores(queries, block_keys, score_scale):
    return (
        jnp.einsum("qhd,khd->hqk", queries, block_keys, preferred_element_type=jnp.float32)
        * score_scale
    )


def per_device(
    inputs,
    gain_one,
    w_query,
    w_key,
    w_value,
    w_out_proj,
    gain_two,
    w_router,
    w_in,
    w_out,
    routes,
    slot_index,
    prompt_of,
    cotangent,
):
    row_count = inputs.shape[1]
    model_width = inputs.shape[2]
    devices = lax.axis_size("expert")
    device = lax.axis_index("expert")
    prompt_rows = NPR * PR_DEV
    prompt_len = PR_DEV * devices
    score_scale = HD ** (-0.5)
    key_block = min(512, prompt_len)
    key_blocks = prompt_len // key_block
    chosen_prompt = prompt_of[0, 0]
    query_pos = device * PR_DEV + jnp.arange(PR_DEV)
    causal = (jnp.arange(CLEN)[None, :] <= jnp.arange(CLEN)[:, None])[None]
    tokens = inputs[0].astype(jnp.float32)
    norm_one = normed(tokens)
    hidden = (norm_one * gain_one).astype(jnp.bfloat16)
    queries = jnp.dot(hidden, w_query, preferred_element_type=jnp.float32).astype(jnp.bfloat16)
    keyset = jnp.dot(hidden, w_key, preferred_element_type=jnp.float32).astype(jnp.bfloat16)
    valueset = jnp.dot(hidden, w_value, preferred_element_type=jnp.float32).astype(jnp.bfloat16)
    query_p = queries[:prompt_rows].reshape(PR_DEV, NPR, H, HD)
    query_c = queries[prompt_rows:].reshape(CLEN, H, HD)
    key_c = keyset[prompt_rows:].reshape(CLEN, H, HD)
    value_c = valueset[prompt_rows:].reshape(CLEN, H, HD)
    key_local = keyset[:prompt_rows].reshape(PR_DEV, NPR, model_width)
    value_local = valueset[:prompt_rows].reshape(PR_DEV, NPR, model_width)
    key_all, value_all = (
        lax.all_gather(key_local, "expert", axis=0, tiled=True),
        lax.all_gather(value_local, "expert", axis=0, tiled=True),
    )

    def take_block(field, offset):
        block_p = lax.dynamic_slice_in_dim(field, offset, key_block, 0).reshape(
            key_block, NPR, H, HD
        )
        return (block_p, lax.dynamic_index_in_dim(block_p, chosen_prompt, 1, keepdims=False))

    def stats_step(block_no, running):
        offset = block_no * key_block
        block_k, block_kc = take_block(key_all, offset)
        affinity_table, visible = prompt_scores(
            query_p, block_k, query_pos, offset + jnp.arange(key_block), score_scale
        )
        return (
            stats_update(running[0], affinity_table, visible),
            stats_update(running[1], cont_scores(query_c, block_kc, score_scale), True),
        )

    start_p = (
        jnp.full((NPR, H, PR_DEV), NEGATIVE, jnp.float32),
        jnp.zeros((NPR, H, PR_DEV), jnp.float32),
    )
    start_c = (jnp.full((H, CLEN), NEGATIVE, jnp.float32), jnp.zeros((H, CLEN), jnp.float32))
    stats_p, stats_c = lax.fori_loop(0, key_blocks, stats_step, (start_p, start_c))
    self_scores = cont_scores(query_c, key_c, score_scale)
    stats_c = stats_update(stats_c, self_scores, causal)
    log_p = stats_p[0] + jnp.log(stats_p[1])
    log_c = stats_c[0] + jnp.log(stats_c[1])

    def output_step(block_no, running):
        offset = block_no * key_block
        block_k, block_kc = take_block(key_all, offset)
        block_v, block_vc = take_block(value_all, offset)
        affinity_table, visible = prompt_scores(
            query_p, block_k, query_pos, offset + jnp.arange(key_block), score_scale
        )
        weight_p = likely(affinity_table, visible, log_p).astype(jnp.bfloat16)
        weight_c = likely(cont_scores(query_c, block_kc, score_scale), True, log_c).astype(
            jnp.bfloat16
        )
        return (
            running[0]
            + jnp.einsum("bhqk,kbhd->qbhd", weight_p, block_v, preferred_element_type=jnp.float32),
            running[1]
            + jnp.einsum("hqk,khd->qhd", weight_c, block_vc, preferred_element_type=jnp.float32),
        )

    zero_p = jnp.zeros((PR_DEV, NPR, H, HD), jnp.float32)
    zero_c = jnp.zeros((CLEN, H, HD), jnp.float32)
    out_p, out_c = lax.fori_loop(0, key_blocks, output_step, (zero_p, zero_c))
    own_weight = likely(self_scores, causal, log_c)
    out_c = out_c + jnp.einsum(
        "hqk,khd->qhd", own_weight.astype(jnp.bfloat16), value_c, preferred_element_type=jnp.float32
    )
    attended32 = jnp.concatenate(
        [out_p.reshape(prompt_rows, model_width), out_c.reshape(CLEN, model_width)], axis=0
    )
    attended = attended32.astype(jnp.bfloat16)
    middle = tokens + jnp.dot(attended, w_out_proj, preferred_element_type=jnp.float32)
    norm_two = normed(middle)
    second = (norm_two * gain_two).astype(jnp.bfloat16)
    logits = jnp.dot(second, w_router, preferred_element_type=jnp.float32)
    expert_count = w_router.shape[1]
    local_experts = w_in.shape[0]
    capacity = max(2, 5 * row_count * TOP // (4 * expert_count))
    route = routes[0]
    slot_now = slot_index[0]
    gates = jax.nn.softmax(jnp.take_along_axis(logits, route, axis=1), axis=-1)
    kept = (slot_now < capacity).astype(jnp.float32)
    target = jnp.where(
        slot_now < capacity, route * capacity + slot_now, expert_count * capacity
    ).reshape(-1)
    fetch_at = jnp.minimum(target, expert_count * capacity - 1)
    weight_pair = gates * kept
    outgoing = (
        jnp.zeros((expert_count * capacity, model_width), jnp.bfloat16)
        .at[target]
        .set(jnp.repeat(second, TOP, axis=0), mode="drop")
    )
    arrived = lax.all_to_all(
        outgoing.reshape(devices, local_experts, capacity, model_width),
        "expert",
        split_axis=0,
        concat_axis=2,
        tiled=True,
    )
    expert_in = arrived.reshape(local_experts, devices * capacity, model_width)
    pre_act = jnp.einsum("erd,edf->erf", expert_in, w_in, preferred_element_type=jnp.float32)
    activated = jax.nn.gelu(pre_act).astype(jnp.bfloat16)
    expert_out = jnp.einsum(
        "erf,efd->erd", activated, w_out, preferred_element_type=jnp.float32
    ).astype(jnp.bfloat16)
    returned = lax.all_to_all(
        expert_out.reshape(1, local_experts, devices * capacity, model_width),
        "expert",
        split_axis=2,
        concat_axis=0,
        tiled=True,
    ).reshape(expert_count * capacity, model_width)
    fetched = jnp.take(returned, fetch_at, axis=0).reshape(row_count, TOP, model_width)
    outputs = (middle + jnp.sum(weight_pair[..., None] * fetched, axis=1)).astype(jnp.bfloat16)
    grad_out = cotangent[0].astype(jnp.float32)
    grad_gates = jnp.sum(grad_out[:, None, :] * fetched, axis=-1) * kept
    grad_pair = (
        (weight_pair[..., None] * grad_out[:, None, :])
        .astype(jnp.bfloat16)
        .reshape(-1, model_width)
    )
    grad_buffer = (
        jnp.zeros((expert_count * capacity, model_width), jnp.bfloat16)
        .at[target]
        .set(grad_pair, mode="drop")
    )
    grad_arrived = lax.all_to_all(
        grad_buffer.reshape(devices, local_experts, capacity, model_width),
        "expert",
        split_axis=0,
        concat_axis=2,
        tiled=True,
    ).reshape(local_experts, devices * capacity, model_width)
    grad_act = jnp.einsum("erd,efd->erf", grad_arrived, w_out, preferred_element_type=jnp.float32)
    grad_pre = gelu_back(pre_act, grad_act).astype(jnp.bfloat16)
    grad_w_out = jnp.einsum(
        "erf,erd->efd", activated, grad_arrived, preferred_element_type=jnp.float32
    )
    grad_w_in = jnp.einsum("erd,erf->edf", expert_in, grad_pre, preferred_element_type=jnp.float32)
    grad_expert_in = jnp.einsum(
        "erf,edf->erd", grad_pre, w_in, preferred_element_type=jnp.float32
    ).astype(jnp.bfloat16)
    grad_returned = lax.all_to_all(
        grad_expert_in.reshape(1, local_experts, devices * capacity, model_width),
        "expert",
        split_axis=2,
        concat_axis=0,
        tiled=True,
    ).reshape(expert_count * capacity, model_width)
    grad_second = jnp.sum(
        kept[..., None]
        * jnp.take(grad_returned, fetch_at, axis=0).reshape(row_count, TOP, model_width),
        axis=1,
    )
    grad_chosen = gates * (grad_gates - jnp.sum(gates * grad_gates, axis=-1, keepdims=True))
    columns = jnp.arange(expert_count)
    grad_logits = jnp.sum(
        (route[..., None] == columns).astype(jnp.float32) * grad_chosen[..., None], axis=1
    ).astype(jnp.bfloat16)
    grad_second = grad_second + jnp.dot(grad_logits, w_router.T, preferred_element_type=jnp.float32)
    grad_router = jnp.dot(second.T, grad_logits, preferred_element_type=jnp.float32)
    grad_gain_two = jnp.sum(grad_second * norm_two, axis=0)
    grad_middle = grad_out + norm_back(middle, grad_second * gain_two)
    grad_attn = grad_middle.astype(jnp.bfloat16)
    grad_out_proj = jnp.dot(attended.T, grad_attn, preferred_element_type=jnp.float32)
    grad_attended = jnp.dot(grad_attn, w_out_proj.T, preferred_element_type=jnp.float32).astype(
        jnp.bfloat16
    )
    delta = jnp.sum(
        (grad_attended.astype(jnp.float32) * attended32).reshape(row_count, H, HD), axis=-1
    )
    delta_p = delta[:prompt_rows].reshape(PR_DEV, NPR, H).transpose(1, 2, 0)
    delta_c = delta[prompt_rows:].T
    grad_o_p = grad_attended[:prompt_rows].reshape(PR_DEV, NPR, H, HD)
    grad_o_c = grad_attended[prompt_rows:].reshape(CLEN, H, HD)
    key_back, value_back = (
        lax.all_gather(key_local, "expert", axis=0, tiled=True),
        lax.all_gather(value_local, "expert", axis=0, tiled=True),
    )
    select = (jnp.arange(NPR) == chosen_prompt).astype(jnp.float32)

    def block_grads(offset):
        block_k, block_kc = take_block(key_back, offset)
        block_v, block_vc = take_block(value_back, offset)
        affinity_table, visible = prompt_scores(
            query_p, block_k, query_pos, offset + jnp.arange(key_block), score_scale
        )
        weight_p = likely(affinity_table, visible, log_p)
        grad_w = jnp.einsum(
            "qbhd,kbhd->bhqk", grad_o_p, block_v, preferred_element_type=jnp.float32
        )
        grad_s = (weight_p * (grad_w - delta_p[..., None])).astype(jnp.bfloat16)
        weight_c = likely(cont_scores(query_c, block_kc, score_scale), True, log_c)
        grad_wc = jnp.einsum("qhd,khd->hqk", grad_o_c, block_vc, preferred_element_type=jnp.float32)
        grad_sc = (weight_c * (grad_wc - delta_c[..., None])).astype(jnp.bfloat16)
        part_qp = (
            jnp.einsum("bhqk,kbhd->qbhd", grad_s, block_k, preferred_element_type=jnp.float32)
            * score_scale
        )
        part_qc = (
            jnp.einsum("hqk,khd->qhd", grad_sc, block_kc, preferred_element_type=jnp.float32)
            * score_scale
        )
        part_kc = (
            jnp.einsum("hqk,qhd->khd", grad_sc, query_c, preferred_element_type=jnp.float32)
            * score_scale
        )
        part_vc = jnp.einsum(
            "hqk,qhd->khd",
            weight_c.astype(jnp.bfloat16),
            grad_o_c,
            preferred_element_type=jnp.float32,
        )
        part_k = (
            jnp.einsum("bhqk,qbhd->kbhd", grad_s, query_p, preferred_element_type=jnp.float32)
            * score_scale
        )
        part_v = jnp.einsum(
            "bhqk,qbhd->kbhd",
            weight_p.astype(jnp.bfloat16),
            grad_o_p,
            preferred_element_type=jnp.float32,
        )
        part_k = part_k + select[None, :, None, None] * part_kc[:, None]
        part_v = part_v + select[None, :, None, None] * part_vc[:, None]
        return (part_qp, part_qc, part_k, part_v)

    def summed_step(block_no, running):
        offset = block_no * key_block
        part_qp, part_qc, part_k, part_v = block_grads(offset)
        stacked = jnp.stack(
            [
                part_k.reshape(key_block, NPR, model_width),
                part_v.reshape(key_block, NPR, model_width),
            ],
            axis=1,
        )
        return (
            running[0] + part_qp,
            running[1] + part_qc,
            lax.dynamic_update_slice_in_dim(running[2], stacked, offset, 0),
        )

    term_init = jnp.zeros((prompt_len, 2, NPR, model_width), jnp.float32)
    grad_qp, grad_qc, term = lax.fori_loop(0, key_blocks, summed_step, (zero_p, zero_c, term_init))
    shares = lax.psum_scatter(
        term.astype(jnp.bfloat16), "expert", scatter_dimension=0, tiled=True
    ).astype(jnp.float32)
    grad_kp = shares[:, 0]
    grad_vp = shares[:, 1]
    grad_self = jnp.einsum("qhd,khd->hqk", grad_o_c, value_c, preferred_element_type=jnp.float32)
    grad_ss = (own_weight * (grad_self - delta_c[..., None])).astype(jnp.bfloat16)
    grad_qc = (
        grad_qc
        + jnp.einsum("hqk,khd->qhd", grad_ss, key_c, preferred_element_type=jnp.float32)
        * score_scale
    )
    grad_kc = (
        jnp.einsum("hqk,qhd->khd", grad_ss, query_c, preferred_element_type=jnp.float32)
        * score_scale
    )
    grad_vc = jnp.einsum(
        "hqk,qhd->khd",
        own_weight.astype(jnp.bfloat16),
        grad_o_c,
        preferred_element_type=jnp.float32,
    )
    grad_q = jnp.concatenate(
        [grad_qp.reshape(prompt_rows, model_width), grad_qc.reshape(CLEN, model_width)], axis=0
    ).astype(jnp.bfloat16)
    grad_k = jnp.concatenate(
        [grad_kp.reshape(prompt_rows, model_width), grad_kc.reshape(CLEN, model_width)], axis=0
    ).astype(jnp.bfloat16)
    grad_v = jnp.concatenate(
        [grad_vp.reshape(prompt_rows, model_width), grad_vc.reshape(CLEN, model_width)], axis=0
    ).astype(jnp.bfloat16)
    grad_query = jnp.dot(hidden.T, grad_q, preferred_element_type=jnp.float32)
    grad_key = jnp.dot(hidden.T, grad_k, preferred_element_type=jnp.float32)
    grad_value = jnp.dot(hidden.T, grad_v, preferred_element_type=jnp.float32)
    grad_hidden = (
        jnp.dot(grad_q, w_query.T, preferred_element_type=jnp.float32)
        + jnp.dot(grad_k, w_key.T, preferred_element_type=jnp.float32)
        + jnp.dot(grad_v, w_value.T, preferred_element_type=jnp.float32)
    )
    grad_gain_one = jnp.sum(grad_hidden * norm_one, axis=0)
    grad_input = grad_middle + norm_back(tokens, grad_hidden * gain_one)
    dense = lax.psum(
        (
            grad_query,
            grad_key,
            grad_value,
            grad_out_proj,
            grad_router,
            grad_gain_one,
            grad_gain_two,
        ),
        ("dp", "expert"),
    )
    expert_sums = (
        lax.psum_scatter(
            grad_w_in.astype(jnp.bfloat16), "dp", scatter_dimension=1, tiled=True
        ).astype(jnp.float32),
        lax.psum_scatter(
            grad_w_out.astype(jnp.bfloat16), "dp", scatter_dimension=1, tiled=True
        ).astype(jnp.float32),
    )
    return (
        outputs[None],
        grad_input[None],
        dense[5],
        dense[0],
        dense[1],
        dense[2],
        dense[3],
        dense[6],
        dense[4],
        expert_sums[0],
        expert_sums[1],
    )


def solution(mesh):
    return jax.shard_map(
        per_device,
        mesh=mesh,
        in_specs=(
            P("dp", "expert", None),
            P(),
            P(),
            P(),
            P(),
            P(),
            P(),
            P(),
            P("expert", None, None),
            P("expert", None, None),
            P("dp", "expert", None),
            P("dp", "expert", None),
            P("dp", "expert"),
            P("dp", "expert", None),
        ),
        out_specs=(
            P("dp", "expert", None),
            P("dp", "expert", None),
            P(),
            P(),
            P(),
            P(),
            P(),
            P(),
            P(),
            P("expert", "dp", None),
            P("expert", "dp", None),
        ),
        check_vma=False,
    )
```

profile of v0, /device:TPU:0, one launch (start us, length us, event | category | flops | bytes accessed | tf_op | source)
XLA Modules:
  0.0 949.1 jit_solution(1461093034648025951)
XLA Ops:
  24.6 24.5 %all-gather.5.cloned.1.call-done = bf16[1024,2,768]{0,2,1:T(8,128)(2,1)} async-done(((bf16[128,2,768]{0,2,1:T(8,128)(2,1)}), bf16[1024,2,768]{0,2,1:T(8,128)(2,1)}) %all-gather.5.cloned.1.call-update) | async-done | bytes 3145744 | tf_op jit(solution)/shard_map/all_gather | solution.py:96
  49.2 11.5 %while.60 = (s32[]{:T(128)}, f32[2,12,128]{2,1,0:T(8,128)S(1)}, f32[2,12,128]{2,1,0:T(8,128)S(1)}, f32[12,128]{1,0:T(8,128)S(1)}, f32[12,128]{1,0:T(8,128)S(1)},...) while((s32[]{:T(128)}, f32[2,12,128]{2,1,0:T(8,128)S(1)}, ...), condition=%wide.region_6.7_spmd.clone, body=%wide.region_1.6_spmd.clone.sunk | while | flops 317021312 | bytes 25410772 | solution.py:122
  61.5 23.0 %all-gather.3.cloned.1.call-done = bf16[1024,2,768]{0,2,1:T(8,128)(2,1)} async-done(((bf16[128,2,768]{0,2,1:T(8,128)(2,1)}), bf16[1024,2,768]{0,2,1:T(8,128)(2,1)}) %all-gather.3.cloned.1.call-update) | async-done | bytes 3145744 | tf_op jit(solution)/shard_map/all_gather | solution.py:97
  84.5 23.2 %while.61 = (s32[]{:T(128)}, f32[128,2,12,64]{0,3,2,1:T(8,128)}, f32[128,12,64]{0,2,1:T(8,128)}, bf16[1024,2,768]{0,2,1:T(8,128)(2,1)}, bf16[1024,2,768]{0,2,1:T...) while((s32[]{:T(128)}, f32[128,2,12,64]{0,3,2,1:T(8,128)}, ...), condition=%wide.region_10.11_spmd.clone, body=%wide.region_9.10_spmd.clone.sunk | while | flops 613286528 | bytes 14117082 | solution.py:148
  91.5 4.3 fusion.279
  102.9 4.5 fusion.279
  118.6 6.6 scatter_custom_fusion
  145.6 6.4 gather_fusion
  153.1 10.7 %scatter_custom_fusion.1 = bf16[960,768]{1,0:T(8,128)(2,1)} fusion(s32[768]{0:T(1024)S(1)} %fusion.141, f32[768,768]{1,0:T(8,128)} %mul.535, f32[768]{0:T(1024)S(1)} %divide_select_fusion, bf16[]{:T(256)} %constant.303.clone.1), kind=kCustom, calls=%fused_computation.162 | custom fusion | flops 1179648 | bytes 3837954 | tf_op jit(solution)/shard_map/scatter | solution.py:210
  171.1 4.5 all-to-all-start.2
  175.6 7.3 fusion.102
  182.9 12.9 %fusion.91 = bf16[1,2,480,768]{3,2,1,0:T(8,128)(2,1)S(1)} fusion(bf16[2,3072,768]{2,1,0:T(8,128)(2,1)} %param.31, f32[2,480,3072]{2,1,0:T(8,128)S(1)} %fusion.102), kind=kOutput, calls=%fused_computation.130 | convolution fusion | flops 4557127680 | bytes 22708224 | tf_op jit(solution)/shard_map/erf,efd->erd/dot_general | solution.py:188
  198.5 4.4 all-to-all-start.1
  202.9 15.3 %fusion.90 = bf16[2,480,3072]{2,1,0:T(8,128)(2,1)S(1)} fusion(f32[2,480,3072]{2,1,0:T(8,128)} %copy-done.6, bf16[2,3072,768]{2,1,0:T(8,128)(2,1)} %param.31, bf16[2,480,768]{2,0,1:T(2,128)(2,1)} %bitcast.22), kind=kOutput, calls=%fused_computation.113 | convolution fusion | flops 4588830720 | bytes 28606464 | tf_op jit(solution)/shard_map/erd,efd->erf/dot_general | solution.py:219
  218.3 9.7 %fusion.92 = bf16[1,2,480,768]{3,2,1,0:T(8,128)(2,1)S(1)} fusion(bf16[2,480,3072]{2,1,0:T(8,128)(2,1)S(1)} %fusion.90, bf16[2,768,3072]{2,1,0:T(8,128)(2,1)} %param.30), kind=kOutput, calls=%fused_computation.131 | convolution fusion | flops 4530585600 | bytes 16809984 | tf_op jit(solution)/shard_map/erf,edf->erd/dot_general | solution.py:225
  230.7 4.4 all-to-all-start.3
  247.9 7.1 all-to-all-done.3
  263.6 4.2 select_convert_fusion
  271.8 4.7 multiply_reduce_fusion.1
  278.7 4.4 reshape.608
  283.1 4.7 multiply_reduce_fusion.2
  297.6 34.8 %while.62 = (s32[]{:T(128)}, f32[128,2,12,64]{0,3,2,1:T(8,128)S(1)}, f32[128,12,64]{0,2,1:T(8,128)S(1)}, bf16[1024,2,2,768]{0,3,2,1:T(8,128)(2,1)}, bf16[1024,2,...) while((s32[]{:T(128)}, ...), condition=%wide.region_24.26_spmd.clone, body=%wide.region_23.25_spmd.clone.sunk | while | flops 1545110144 | bytes 120585592 | solution.py:330
  332.4 8.7 copy.218
  342.5 10.6 %convolution_convert_fusion.1 = bf16[2,768,3072]{2,1,0:T(8,128)(2,1)} fusion(bf16[2,480,3072]{2,1,0:T(8,128)(2,1)} %copy-done.83, bf16[2,480,768]{2,0,1:T(2,128)(2,1)S(1)} %bitcast.375), kind=kOutput, calls=%fused_computation.116 | convolution fusion | flops 4534566912 | bytes 16809984 | tf_op jit(solution)/shard_map/erd,erf->edf/dot_general | solution.py:224
  353.1 12.6 %convolution_convert_fusion = bf16[2,3072,768]{2,1,0:T(8,128)(2,1)} fusion(bf16[2,480,768]{2,0,1:T(2,128)(2,1)} %bitcast.22, f32[2,480,3072]{2,1,0:T(8,128)} %copy-done.6), kind=kOutput, calls=%fused_computation.115 | convolution fusion | flops 4561108992 | bytes 22708224 | tf_op jit(solution)/shard_map/erf,erd->efd/dot_general | solution.py:221
  376.9 25.3 %reduce-scatter.10.cloned.1.call-done = bf16[128,3072]{1,0:T(8,128)(2,1)} async-done(((bf16[1024,3072]{1,0:T(8,128)(2,1)}), bf16[128,3072]{1,0:T(8,128)(2,1)}) %reduce-scatter.10.cloned.1.call-update) | async-done | bytes 786448
  420.8 47.0 %all-reduce = (f32[768]{0:T(1024)}, f32[768]{0:T(1024)}, f32[768,16]{0,1:T(8,128)}) all-reduce(f32[768]{0:T(1024)S(1)} %get-tuple-element.1189, f32[768]{0:T(1024)S(1)} %copy-done.79, f32[768,16]{0,1:T(8,128)S(1)} %copy-done.64), channel_id=1, replica_groups=mesh['dp'=4,'expert'=8] {'dp','expert'}, use_global_device_ids=true, to_apply=%region_28.30 | all-reduce | flops 13824 | bytes 110592 | tf_op jit(solution)/shard_map/psum | solution.py:372
  470.4 96.4 %reduce-scatter.6.cloned.1.call-done = bf16[2,192,3072]{2,1,0:T(8,128)(2,1)} async-done(((bf16[2,768,3072]{2,1,0:T(8,128)(2,1)}), bf16[2,192,3072]{2,1,0:T(8,128)(2,1)}) %reduce-scatter.6.cloned.1.call-update) | async-done | bytes 2359312 | tf_op jit(solution)/shard_map/reduce_scatter | solution.py:385
  566.9 4.4 convert_element_type.203
  571.3 160.1 %reduce-scatter.8.cloned.1.call-done = bf16[2,768,768]{2,1,0:T(8,128)(2,1)} async-done(((bf16[2,3072,768]{2,1,0:T(8,128)(2,1)}), bf16[2,768,768]{2,1,0:T(8,128)(2,1)}) %reduce-scatter.8.cloned.1.call-update) | async-done | bytes 2359312 | tf_op jit(solution)/shard_map/reduce_scatter | solution.py:388
  731.4 4.2 convert_element_type.205
  735.6 196.4 %all-reduce.4.cloned.1.call-done = (f32[768,768]{1,0:T(8,128)}, f32[768,768]{1,0:T(8,128)}, f32[768,768]{1,0:T(8,128)}, f32[768,768]{1,0:T(8,128)}) async-done(((f32[768,768]{1,0:T(8,128)}, f32[768,768]{1,0:T(8,128)}, f32[768,768]{1,0:T(8,128)}, f32[768,768]{1,0:T(8,128)}), (f32[768,768]{1,0:T(8,128)}, f32[768,768]{1,0:T(8,128)}, f32[768,768]{1,0:T(8,128)}, ...) | async-done | bytes 9437200 | tf_op jit(solution)/shard_map/psum | solution.py:372
  (404 shorter events, 202.1 us)
Async XLA Ops:
  7.2 107.3 %copy-start = (bf16[768,768]{1,0:T(8,128)(2,1)S(1)}, bf16[768,768]{1,0:T(8,128)(2,1)}, u32[]{:S(2)}) copy-start(bf16[768,768]{1,0:T(8,128)(2,1)} %param.27) | copy-start | bytes 3538948
  7.2 42.0 %all-gather.5.cloned.1.call-start = ((), (), s32[]{:S(2)}) async-start(), calls=%async_computation.8 | async-start | bytes 3538944 | tf_op jit(solution)/shard_map/all_gather | solution.py:96
  9.2 8.5 copy-start.70
  13.5 71.0 %all-gather.3.cloned.1.call-start = ((), (), s32[]{:S(2)}) async-start(), calls=%async_computation.7 | async-start | bytes 3538944 | tf_op jit(solution)/shard_map/all_gather | solution.py:97
  17.7 43.0 %copy-start.62 = (pred[128,128]{0,1:T(8,128)(4,1)}, pred[128,128]{0,1:T(8,128)(4,1)S(1)}, u32[]{:S(2)}) copy-start(pred[128,128]{0,1:T(8,128)(4,1)S(1)} %iota_compare_fusion) | copy-start | bytes 49156
  22.7 85.0 %copy-start.43 = (bf16[128,768]{0,1:T(8,128)(2,1)}, bf16[128,768]{0,1:T(8,128)(2,1)S(1)}, u32[]{:S(2)}) copy-start(bf16[128,768]{0,1:T(8,128)(2,1)S(1)} %copy.168) | copy-start | bytes 589828
  24.6 36.1 %copy-start.11 = (f32[12,128,128]{1,2,0:T(8,128)}, f32[12,128,128]{1,2,0:T(8,128)S(1)}, u32[]{:S(2)}) copy-start(f32[12,128,128]{1,2,0:T(8,128)S(1)} %get-tuple-element.1297) | copy-start | bytes 2359300
  107.6 4.8 copy-start.2
  107.7 4.8 copy-start.4
  107.7 4.8 copy-start.48
  109.6 4.9 copy-start.28
  116.6 28.7 %copy-start.23 = (bf16[384,768]{1,0:T(8,128)(2,1)}, bf16[384,768]{1,0:T(8,128)(2,1)S(1)}, u32[]{:S(2)}) copy-start(bf16[384,768]{1,0:T(8,128)(2,1)S(1)} %multiply_convert_fusion.4) | copy-start | bytes 1769476
  130.5 40.6 %all-to-all-start = ((bf16[8,2,60,768]{3,1,2,0:T(2,128)(2,1)}), bf16[8,2,60,768]{3,1,2,0:T(2,128)(2,1)S(1)}, u32[]{:S(2)}, u32[]{:S(2)}) async-start(bf16[8,2,60,768]{3,1,2,0:T(2,128)(2,1)} %copy.179), calls=%async_computation | async-start | bytes 2949120 | tf_op jit(solution)/shard_map/all_to_all | solution.py:178
  134.7 17.6 %copy-start.25 = (s32[1,384,2]{2,1,0:T(8,128)}, s32[1,384,2]{2,1,0:T(8,128)S(1)}, u32[]{:S(2)}) copy-start(s32[1,384,2]{2,1,0:T(8,128)S(1)} %copy.172) | copy-start | bytes 9220
  152.1 11.7 %copy-start.34 = (f32[384,2]{1,0:T(8,128)}, f32[384,2]{1,0:T(8,128)S(1)}, u32[]{:S(2)}) copy-start(f32[384,2]{1,0:T(8,128)S(1)} %reshape.630) | copy-start | bytes 9220
  171.1 11.8 %copy-start.18 = (bf16[8,2,60,768]{3,1,2,0:T(2,128)(2,1)}, bf16[8,2,60,768]{3,1,2,0:T(2,128)(2,1)S(1)}, u32[]{:S(2)}) copy-start(bf16[8,2,60,768]{3,1,2,0:T(2,128)(2,1)S(1)} %all-to-all-done) | copy-start | bytes 4423684
  171.1 27.4 %all-to-all-start.2 = ((bf16[8,2,60,768]{3,1,2,0:T(2,128)(2,1)}), bf16[8,2,60,768]{3,1,2,0:T(2,128)(2,1)}, u32[]{:S(2)}, u32[]{:S(2)}) async-start(bf16[8,2,60,768]{3,1,2,0:T(2,128)(2,1)} %copy.183), calls=%async_computation.2 | async-start | bytes 2949120 | tf_op jit(solution)/shard_map/all_to_all | solution.py:212
  182.9 13.0 %copy-start.6 = (f32[2,480,3072]{2,1,0:T(8,128)}, f32[2,480,3072]{2,1,0:T(8,128)S(1)}, u32[]{:S(2)}) copy-start(f32[2,480,3072]{2,1,0:T(8,128)S(1)} %fusion.102) | copy-start | bytes 35389444
  198.5 32.1 %all-to-all-start.1 = ((bf16[1,2,480,768]{3,1,0,2:T(2,128)(2,1)}), bf16[1,2,480,768]{3,1,0,2:T(2,128)(2,1)S(1)}, u32[]{:S(2)}, u32[]{:S(2)}) async-start(bf16[1,2,480,768]{3,1,0,2:T(2,128)(2,1)} %copy.181), calls=%async_computation.1 | async-start | bytes 2949120 | tf_op jit(solution)/shard_map/all_to_all | solution.py:191
  218.3 9.8 %copy-start.83 = (bf16[2,480,3072]{2,1,0:T(8,128)(2,1)}, bf16[2,480,3072]{2,1,0:T(8,128)(2,1)S(1)}, u32[]{:S(2)}) copy-start(bf16[2,480,3072]{2,1,0:T(8,128)(2,1)S(1)} %fusion.90) | copy-start | bytes 17694724
  230.7 24.4 %all-to-all-start.3 = ((bf16[1,2,480,768]{3,1,0,2:T(2,128)(2,1)}), bf16[1,2,480,768]{3,1,0,2:T(2,128)(2,1)}, u32[]{:S(2)}, u32[]{:S(2)}) async-start(bf16[1,2,480,768]{3,1,0,2:T(2,128)(2,1)} %copy.185), calls=%async_computation.3 | async-start | bytes 2949120 | tf_op jit(solution)/shard_map/all_to_all | solution.py:228
  235.1 167.1 %reduce-scatter.10.cloned.1.call-start = ((), (), s32[]{:S(2)}) async-start(), calls=%async_computation.11 | async-start | bytes 7077888
  283.1 4.7 copy-start.32
  283.1 4.7 copy-start.36
  305.4 6.5 slice-start
  307.1 4.8 slice-start.1
  322.8 6.5 slice-start
  324.5 4.8 slice-start.1
  341.1 225.7 %reduce-scatter.6.cloned.1.call-start = ((), (), s32[]{:S(2)}) async-start(), calls=%async_computation.9 | async-start | bytes 11796480 | tf_op jit(solution)/shard_map/reduce_scatter | solution.py:385
  353.1 378.3 %reduce-scatter.8.cloned.1.call-start = ((), (), s32[]{:S(2)}) async-start(), calls=%async_computation.10 | async-start | bytes 11796480 | tf_op jit(solution)/shard_map/reduce_scatter | solution.py:388
  365.8 566.2 %all-reduce.4.cloned.1.call-start = ((), (), s32[]{:S(2)}) async-start(), calls=%async_computation.12 | async-start | bytes 18874368 | tf_op jit(solution)/shard_map/psum | solution.py:372
  419.0 48.8 %copy-start.78 = (f32[384]{0:T(512)S(1)}, f32[384]{0:T(512)}, u32[]{:S(2)}) copy-start(f32[384]{0:T(512)} %copy-done.77) | copy-start | bytes 4612
  (69 other events, 156.1 us)
Sparse Core Ops, SparseCore 0:
  13.6 35.5 all-gather.4
  51.6 32.8 all-gather.2
  341.2 60.9 reduce-scatter.9
  404.5 162.2 reduce-scatter.5
  569.2 162.1 reduce-scatter.7
  739.1 192.8 all-reduce.3
where the time goes:
time: 960 us; the launch traced here: 949 us
  waiting for transfers between devices  533 us (56%)
  local copies, waits for them, and re-layouts  141 us (15%)
  matrix products  140 us (15%)
  other arithmetic  53.3 us (6%)
  blocking collectives  47 us (5%)
  starting transfers between devices  17.5 us (2%)
  between operations  16.7 us (2%)
    psum x1, waiting for transfers between devices, per_device(): lax.psum((grad_query, grad_key, grad_value, grad_out_proj, grad_router, g...  196 us
    reduce_scatter x1, waiting for transfers between devices, per_device(): lax.psum_scatter(grad_w_out.astype(jnp.bfloat16), 'dp', scatter_dimension...  160 us
    reduce_scatter x1, waiting for transfers between devices, per_device(): lax.psum_scatter(grad_w_in.astype(jnp.bfloat16), 'dp', scatter_dimension=...  96.4 us
    psum x1, blocking collectives, per_device(): lax.psum((grad_query, grad_key, grad_value, grad_out_proj, grad_router, g...  47 us
    unnamed x177, local copies, waits for them, and re-layouts  30.5 us
    unnamed x7, waiting for transfers between devices  25.4 us
    all_gather x1, waiting for transfers between devices, per_device(): lax.all_gather(key_local, 'expert', axis=0, tiled=True)  24.5 us
    all_gather x1, waiting for transfers between devices, per_device(): lax.all_gather(value_local, 'expert', axis=0, tiled=True)  23 us
  transfers between devices with their start and end apart: 10, of which 7 were waited for; matrix products, arithmetic and copies ran while one was open for 19% of the time, Pallas kernels for 0%

commit v1 on v0

v1 whole, which is shorter than its diff:
```python
import functools

import jax
import jax.numpy as jnp
from jax import lax
from jax.experimental import pallas as pl
from jax.experimental.pallas import tpu as pltpu
from jax.sharding import PartitionSpec as P

H = 12
HD = 64
TOP = 2
NPR = 2
CLEN = 128
PR_DEV = 128
PAIR = 2 * HD
TWO = 2 * PR_DEV

NEGATIVE = -1e30
BF = jnp.bfloat16
F32 = jnp.float32
SCALE = HD ** (-0.5)

NN = ((1,), (0,))
NT = ((1,), (1,))
TN = ((0,), (0,))


def dot(a, b, dims=NN, out=F32):
    return lax.dot_general(a, b, (dims, ((), ())), preferred_element_type=out)


def iota(shape, dim):
    return lax.broadcasted_iota(jnp.int32, shape, dim)


def fill_bias(bias_ref, device, blocks):
    for m in range(blocks):
        offset = (jnp.bitwise_xor(device, m) - device) * PR_DEV
        seen = iota((PR_DEV, PR_DEV), 0) + offset <= iota((PR_DEV, PR_DEV), 1)
        bias_ref[m * PR_DEV : (m + 1) * PR_DEV, :] = jnp.where(seen, 0.0, NEGATIVE)


def two_heads(rows):
    keep = (iota((TWO, PAIR), 0) < PR_DEV) == (iota((TWO, PAIR), 1) < HD)
    return jnp.where(keep, jnp.concatenate([rows, rows], axis=0), jnp.zeros((), rows.dtype))


def join_heads(both):
    first = iota((PAIR, PR_DEV), 0) < HD
    return jnp.where(first, both[:, :PR_DEV], both[:, PR_DEV:]).T


def twice(block):
    return jnp.concatenate([block, block], axis=1)


def attention_forward_kernel(info, q_ref, k_ref, v_ref, kc_ref, vc_ref, o_ref, lse_ref, bias_ref):
    blocks = k_ref.shape[0]
    keys = blocks * PR_DEV
    device, chosen = info[0], info[1]

    @pl.when(pl.program_id(0) == 0)
    def _():
        fill_bias(bias_ref, device, blocks)

    for group in range(3):
        rows = slice(group * PR_DEV, (group + 1) * PR_DEV)
        q2 = two_heads(q_ref[rows, :] * jnp.asarray(SCALE, BF))
        which = group if group < NPR else chosen
        k = k_ref[:, which].reshape(keys, PAIR)
        v = v_ref[:, which].reshape(keys, PAIR)
        st = dot(k, q2, NT)
        if group < NPR:
            st = st + twice(bias_ref[...])
            top = jnp.max(st, axis=0, keepdims=True)
            p = jnp.exp(st - top)
            total = jnp.sum(p, axis=0, keepdims=True)
            both = dot(v, p.astype(BF), TN)
        else:
            own = dot(kc_ref[...], q2, NT) + twice(bias_ref[:PR_DEV, :])
            top = jnp.maximum(
                jnp.max(st, axis=0, keepdims=True), jnp.max(own, axis=0, keepdims=True)
            )
            p = jnp.exp(st - top)
            p_own = jnp.exp(own - top)
            total = jnp.sum(p, axis=0, keepdims=True) + jnp.sum(p_own, axis=0, keepdims=True)
            both = dot(v, p.astype(BF), TN) + dot(vc_ref[...], p_own.astype(BF), TN)
        both = both * (1.0 / total)
        o_ref[rows, :] = join_heads(both).astype(BF)
        lse_ref[0, group : group + 1, :] = top + jnp.log(total)


def attention_backward_kernel(
    info, q_ref, k_ref, v_ref, kc_ref, vc_ref, do_ref, lse_ref,
    dq_ref, dk_ref, dv_ref, dkc_ref, dvc_ref, bias_ref, dk_acc, dv_acc,
):
    blocks = k_ref.shape[0]
    keys = blocks * PR_DEV
    device, chosen = info[0], info[1]

    @pl.when(pl.program_id(0) == 0)
    def _():
        fill_bias(bias_ref, device, blocks)

    for group in range(3):
        rows = slice(group * PR_DEV, (group + 1) * PR_DEV)
        q2 = two_heads(q_ref[rows, :] * jnp.asarray(SCALE, BF))
        do2 = two_heads(do_ref[rows, :])
        lse = lse_ref[0, group : group + 1, :]
        which = group if group < NPR else chosen
        k = k_ref[:, which].reshape(keys, PAIR)
        v = v_ref[:, which].reshape(keys, PAIR)
        st = dot(k, q2, NT)
        if group < NPR:
            st = st + twice(bias_ref[...])
        p = jnp.exp(st - lse)
        dp = dot(v, do2, NT)
        delta = jnp.sum(p * dp, axis=0, keepdims=True)
        if group == NPR:
            kc, vc = kc_ref[...], vc_ref[...]
            p_own = jnp.exp(dot(kc, q2, NT) + twice(bias_ref[:PR_DEV, :]) - lse)
            dp_own = dot(vc, do2, NT)
            delta = delta + jnp.sum(p_own * dp_own, axis=0, keepdims=True)
        ds = (p * (dp - delta)).astype(BF)
        dk = dot(ds, q2)
        dv = dot(p.astype(BF), do2)
        dq = dot(k, ds, TN)
        if group < NPR:
            dk_acc[:, group] = dk.reshape(blocks, PR_DEV, PAIR)
            dv_acc[:, group] = dv.reshape(blocks, PR_DEV, PAIR)
        else:
            ds_own = (p_own * (dp_own - delta)).astype(BF)
            dq = dq + dot(kc, ds_own, TN)
            dkc_ref[...] = dot(ds_own, q2).astype(BF)
            dvc_ref[...] = dot(p_own.astype(BF), do2).astype(BF)
            dk_acc[:, chosen] += dk.reshape(blocks, PR_DEV, PAIR)
            dv_acc[:, chosen] += dv.reshape(blocks, PR_DEV, PAIR)
        dq_ref[rows, :] = (join_heads(dq) * SCALE).astype(BF)
    dk_ref[...] = dk_acc[...].astype(BF)
    dv_ref[...] = dv_acc[...].astype(BF)


def attention_specs(blocks, rows):
    q_spec = pl.BlockSpec((rows, PAIR), lambda h, info: (0, h))
    k_spec = pl.BlockSpec((blocks, NPR, PR_DEV, PAIR), lambda h, info: (0, 0, 0, h))
    c_spec = pl.BlockSpec((CLEN, PAIR), lambda h, info: (0, h))
    l_spec = pl.BlockSpec((1, 3, TWO), lambda h, info: (h, 0, 0))
    return q_spec, k_spec, c_spec, l_spec


def attention_forward(info, q, k, v, kc, vc):
    blocks, rows, pairs = k.shape[0], q.shape[0], q.shape[1] // PAIR
    q_spec, k_spec, c_spec, l_spec = attention_specs(blocks, rows)
    flops = pairs * 3 * 4 * TWO * blocks * PR_DEV * PAIR
    return pl.pallas_call(
        attention_forward_kernel,
        grid_spec=pltpu.PrefetchScalarGridSpec(
            num_scalar_prefetch=1,
            grid=(pairs,),
            in_specs=[q_spec, k_spec, k_spec, c_spec, c_spec],
            out_specs=[q_spec, l_spec],
            scratch_shapes=[pltpu.VMEM((blocks * PR_DEV, PR_DEV), F32)],
        ),
        out_shape=[
            jax.ShapeDtypeStruct(q.shape, BF),
            jax.ShapeDtypeStruct((pairs, 3, TWO), F32),
        ],
        compiler_params=pltpu.CompilerParams(vmem_limit_bytes=56 * 1024 * 1024),
        cost_estimate=pl.CostEstimate(flops=4 * flops, bytes_accessed=2 * k.size * 2, transcendentals=0),
        name="attention_forward",
    )(info, q, k, v, kc, vc)


def attention_backward(info, q, k, v, kc, vc, do, lse):
    blocks, rows, pairs = k.shape[0], q.shape[0], q.shape[1] // PAIR
    q_spec, k_spec, c_spec, l_spec = attention_specs(blocks, rows)
    flops = pairs * 3 * 10 * TWO * blocks * PR_DEV * PAIR
    return pl.pallas_call(
        attention_backward_kernel,
        grid_spec=pltpu.PrefetchScalarGridSpec(
            num_scalar_prefetch=1,
            grid=(pairs,),
            in_specs=[q_spec, k_spec, k_spec, c_spec, c_spec, q_spec, l_spec],
            out_specs=[q_spec, k_spec, k_spec, c_spec, c_spec],
            scratch_shapes=[
                pltpu.VMEM((blocks * PR_DEV, PR_DEV), F32),
                pltpu.VMEM((blocks, NPR, PR_DEV, PAIR), F32),
                pltpu.VMEM((blocks, NPR, PR_DEV, PAIR), F32),
            ],
        ),
        out_shape=[
            jax.ShapeDtypeStruct(q.shape, BF),
            jax.ShapeDtypeStruct(k.shape, BF),
            jax.ShapeDtypeStruct(k.shape, BF),
            jax.ShapeDtypeStruct(kc.shape, BF),
            jax.ShapeDtypeStruct(kc.shape, BF),
        ],
        compiler_params=pltpu.CompilerParams(vmem_limit_bytes=60 * 1024 * 1024),
        cost_estimate=pl.CostEstimate(flops=4 * flops, bytes_accessed=4 * k.size * 2, transcendentals=0),
        name="attention_backward",
    )(info, q, k, v, kc, vc, do, lse)


def swap(value, axis, mask):
    size = lax.axis_size(axis)
    return lax.ppermute(value, axis, [(i, i ^ mask) for i in range(size)])


def gather_relative(own, axis):
    size = lax.axis_size(axis)
    chips = [own] + [swap(own, axis, mask) for mask in range(2, size, 2)]
    stacked = jnp.stack(chips)
    other = swap(stacked, axis, 1)
    return jnp.stack([stacked, other], axis=1).reshape((size,) + own.shape)


def scatter_relative(parts, axis):
    size = lax.axis_size(axis)
    halves = parts.reshape((size // 2, 2) + parts.shape[1:])
    came = swap(halves[:, 1], axis, 1)
    summed = (halves[:, 0].astype(F32) + came.astype(F32)).astype(BF)
    total = summed[0].astype(F32)
    for chip in range(1, size // 2):
        total = total + swap(summed[chip], axis, 2 * chip).astype(F32)
    return total


def at(value, index):
    return lax.dynamic_index_in_dim(value, index, 0, keepdims=False)


def all_reduce(rows):
    dp, size = lax.axis_size("dp"), lax.axis_size("expert")
    z, e = lax.axis_index("dp"), lax.axis_index("expert")
    chips = size // 2
    core, chip = lax.rem(e, 2), lax.div(e, 2)
    width = rows.shape[1]
    part = rows.shape[0] // (dp * size)
    value = rows.reshape(2, chips, dp, part, width)
    value = (at(value, core).astype(F32) + swap(at(value, 1 - core), "expert", 1).astype(F32)).astype(BF)
    total = at(value, chip).astype(F32)
    for m in range(1, chips):
        total = total + swap(at(value, jnp.bitwise_xor(chip, m)), "expert", 2 * m).astype(F32)
    value = total.astype(BF)
    total = at(value, z).astype(F32)
    for m in range(1, dp):
        total = total + swap(at(value, jnp.bitwise_xor(z, m)), "dp", m).astype(F32)
    own = total.astype(BF)

    def spread(own, axis, index, count, step):
        full = jnp.zeros((count,) + own.shape, own.dtype)
        full = lax.dynamic_update_index_in_dim(full, own, index, 0)
        for m in range(1, count):
            full = lax.dynamic_update_index_in_dim(
                full, swap(own, axis, m * step), jnp.bitwise_xor(index, m), 0
            )
        return full

    own = spread(own, "dp", z, dp, 1)
    own = spread(own, "expert", chip, chips, 2)
    own = spread(own, "expert", core, 2, 1)
    return own.reshape(rows.shape)


def to_experts(slots):
    return lax.all_to_all(slots, "expert", split_axis=0, concat_axis=0, tiled=True)


def gelu_parts(a):
    inner = 0.7978845608 * (a + 0.044715 * a * a * a)
    t = jnp.tanh(inner)
    value = 0.5 * a * (1.0 + t)
    slope = 0.5 * (1.0 + t) + 0.5 * a * (1.0 - t * t) * (
        0.7978845608 * (1.0 + 3.0 * 0.044715 * a * a)
    )
    return value, slope


def root(values):
    return lax.rsqrt(jnp.mean(values * values, axis=-1, keepdims=True) + 1e-06)


def norm_back(norm, scale, grad):
    return scale * (grad - norm * jnp.mean(grad * norm, axis=-1, keepdims=True))


def per_device(
    inputs,
    gain_one,
    w_query,
    w_key,
    w_value,
    w_out_proj,
    gain_two,
    w_router,
    w_in,
    w_out,
    routes,
    slot_index,
    prompt_of,
    cotangent,
):
    row_count, width = inputs.shape[1], inputs.shape[2]
    dp, devices = lax.axis_size("dp"), lax.axis_size("expert")
    z, device = lax.axis_index("dp"), lax.axis_index("expert")
    prompt_rows = NPR * PR_DEV
    expert_count, local = w_router.shape[1], w_in.shape[0]
    hidden_units = w_in.shape[2]
    capacity = max(2, 5 * row_count * TOP // (4 * expert_count))
    room = -(-capacity // 16) * 16
    slots = expert_count * room
    info = jnp.stack([device, prompt_of[0, 0]]).astype(jnp.int32)

    row = jnp.arange(row_count)
    source = jnp.where(row < prompt_rows, (row % PR_DEV) * NPR + row // PR_DEV, row)
    order = (source[:, None] == jnp.arange(row_count)[None, :]).astype(BF)
    tokens = dot(order, inputs[0])
    cot = dot(order, cotangent[0])
    cot_low = cot.astype(BF)
    table = jnp.concatenate([routes[0], slot_index[0]], axis=1).astype(BF)
    table_rows = dot(table, order, ((0,), (1,)))
    table_cols = dot(order, table)

    scale_one = root(tokens)
    norm_one = tokens * scale_one
    hidden = (norm_one * gain_one).astype(BF)
    hidden_all = gather_relative(hidden[:prompt_rows], "expert")
    hidden_all = hidden_all.reshape(devices * prompt_rows, width)
    key_all = dot(hidden_all, w_key).astype(BF).reshape(devices, NPR, PR_DEV, width)
    value_all = dot(hidden_all, w_value).astype(BF).reshape(devices, NPR, PR_DEV, width)
    queries = dot(hidden, w_query).astype(BF)
    hidden_c = hidden[prompt_rows:]
    key_c = dot(hidden_c, w_key).astype(BF)
    value_c = dot(hidden_c, w_value).astype(BF)
    attended, lse = attention_forward(info, queries, key_all, value_all, key_c, value_c)

    message = jnp.concatenate(
        [cot_low, jnp.pad(table_rows.astype(BF), ((0, 12), (0, width - row_count)))], axis=0
    )
    cots, tables = [cot_low], [table_rows]
    for m in range(1, dp):
        came = swap(message, "dp", m)
        cots.append(came[:row_count])
        tables.append(came[row_count : row_count + 4, :row_count].astype(F32))

    slot_no = jnp.arange(slots, dtype=F32)[:, None]

    def choices(rows):
        picks = []
        for k in range(TOP):
            target = jnp.where(rows[TOP + k] < capacity, rows[k] * room + rows[TOP + k], -1.0)
            picks.append((slot_no == target[None, :]).astype(BF))
        return picks

    picks = [choices(rows) for rows in tables]
    pick_any = [a + b for a, b in picks]
    others = jnp.stack(
        [
            jnp.sum(a.astype(F32) * rows[1][None, :] + b.astype(F32) * rows[0][None, :], axis=1)
            for (a, b), rows in zip(picks, tables)
        ]
    )
    others = others.reshape(dp, devices, local * room).transpose(1, 0, 2)
    others = to_experts(others).reshape(devices, dp, local, room)
    others = others.transpose(1, 2, 0, 3).reshape(dp, local, devices * room, 1)

    def dispatch(pick, values):
        outgoing = dot(pick, values, out=F32).astype(BF).reshape(devices, local * room, width)
        arrived = to_experts(outgoing).reshape(devices, local, room, width)
        return arrived.transpose(1, 0, 2, 3).reshape(local, devices * room, width)

    cot_slots = [dispatch(pick, values) for pick, values in zip(pick_any, cots)]

    middle = tokens + dot(attended, w_out_proj)
    scale_two = root(middle)
    norm_two = middle * scale_two
    second = (norm_two * gain_two).astype(BF)
    logits = dot(second, w_router)
    columns = jnp.arange(expert_count, dtype=F32)[None, :]
    chosen = [table_cols[:, k : k + 1] == columns for k in range(TOP)]
    chosen_logits = [jnp.sum(jnp.where(c, logits, 0.0), axis=1, keepdims=True) for c in chosen]
    gate0 = jax.nn.sigmoid(chosen_logits[0] - chosen_logits[1])
    gate1 = jax.nn.sigmoid(chosen_logits[1] - chosen_logits[0])

    def gate_of(rows_in, other, expert):
        own_logits = dot(rows_in, w_router)
        mine = jnp.sum(jnp.where(columns == expert, own_logits, 0.0), axis=1, keepdims=True)
        theirs = jnp.sum(jnp.where(columns == other, own_logits, 0.0), axis=1, keepdims=True)
        return jax.nn.sigmoid(mine - theirs)

    def weighted(rows_in, other, cot_rows):
        return jnp.stack(
            [
                (
                    gate_of(rows_in[l], other[l], (device * local + l).astype(F32))
                    * cot_rows[l].astype(F32)
                ).astype(BF)
                for l in range(local)
            ]
        )

    expert_in = dispatch(pick_any[0], second)
    grad_expert = weighted(expert_in, others[0], cot_slots[0])
    pre_act = jnp.einsum("erd,edf->erf", expert_in, w_in, preferred_element_type=F32)
    active, slope = gelu_parts(pre_act)
    expert_out = jnp.einsum(
        "erf,efd->erd", active.astype(BF), w_out, preferred_element_type=F32
    ).astype(BF)

    def back(rows_out):
        outgoing = rows_out.reshape(local, devices, room, width).transpose(1, 0, 2, 3)
        return to_experts(outgoing.reshape(devices, local * room, width)).reshape(slots, width)

    returned = back(expert_out)
    grad_act = jnp.einsum("erd,efd->erf", grad_expert, w_out, preferred_element_type=F32)
    grad_pre = (grad_act * slope).astype(BF)
    grad_in = jnp.einsum("erf,edf->erd", grad_pre, w_in, preferred_element_type=F32).astype(BF)
    grad_returned = back(grad_in)

    ins, grads = [expert_in], [grad_expert]
    for m in range(1, dp):
        rows_in = dispatch(pick_any[m], swap(second, "dp", m))
        ins.append(rows_in)
        grads.append(weighted(rows_in, others[m], cot_slots[m]))
    all_in = jnp.concatenate(ins, axis=1)
    all_grad = jnp.concatenate(grads, axis=1)
    part = hidden_units // dp
    w_in_part = lax.dynamic_slice_in_dim(w_in, z * part, part, 2)
    w_out_part = lax.dynamic_slice_in_dim(w_out, z * part, part, 1)
    pre_part = jnp.einsum("erd,edf->erf", all_in, w_in_part, preferred_element_type=F32)
    active_part, slope_part = gelu_parts(pre_part)
    grad_act_part = jnp.einsum("erd,efd->erf", all_grad, w_out_part, preferred_element_type=F32)
    grad_pre_part = (grad_act_part * slope_part).astype(BF)
    grad_w_in = jnp.einsum("erd,erf->edf", all_in, grad_pre_part, preferred_element_type=F32)
    grad_w_out = jnp.einsum(
        "erf,erd->efd", active_part.astype(BF), all_grad, preferred_element_type=F32
    )
    share = width // dp
    grad_w_in = grad_w_in.astype(BF).reshape(local, dp, share, part)
    grad_w_in = lax.all_to_all(
        grad_w_in.transpose(1, 0, 2, 3), "dp", split_axis=0, concat_axis=0, tiled=True
    )
    grad_w_in = grad_w_in.transpose(1, 2, 0, 3).reshape(local, share, hidden_units).astype(F32)

    fetched = [dot(pick, returned, TN) for pick in picks[0]]
    outputs = (middle + (gate0 * fetched[0] + gate1 * fetched[1])).astype(BF)
    outputs = dot(order, outputs, TN).astype(BF)
    grad_gate0 = jnp.sum(cot * fetched[0], axis=1, keepdims=True)
    grad_gate1 = jnp.sum(cot * fetched[1], axis=1, keepdims=True)
    mean_gate = gate0 * grad_gate0 + gate1 * grad_gate1
    grad_logits = (
        jnp.where(chosen[0], gate0 * (grad_gate0 - mean_gate), 0.0)
        + jnp.where(chosen[1], gate1 * (grad_gate1 - mean_gate), 0.0)
    ).astype(BF)
    grad_second = dot(pick_any[0], grad_returned, TN) + dot(grad_logits, w_router, NT)
    grad_router_t = dot(grad_logits, second, TN)
    grad_gain_two = jnp.sum(grad_second * norm_two, axis=0, keepdims=True)
    grad_middle = cot + norm_back(norm_two, scale_two, grad_second * gain_two)
    grad_attn = grad_middle.astype(BF)
    grad_out_proj = dot(attended, grad_attn, TN)
    grad_attended = dot(grad_attn, w_out_proj, NT).astype(BF)

    grad_q, part_k, part_v, grad_kc, grad_vc = attention_backward(
        info, queries, key_all, value_all, key_c, value_c, grad_attended, lse
    )
    part_k = part_k.reshape(devices * prompt_rows, width)
    part_v = part_v.reshape(devices * prompt_rows, width)
    grad_query = dot(hidden, grad_q, TN)
    grad_key = dot(hidden_all, part_k, TN) + dot(hidden_c, grad_kc, TN)
    grad_value = dot(hidden_all, part_v, TN) + dot(hidden_c, grad_vc, TN)
    part_hidden = (dot(part_k, w_key, NT) + dot(part_v, w_value, NT)).astype(BF)
    share_hidden = scatter_relative(part_hidden.reshape(devices, prompt_rows, width), "expert")
    grad_hidden = dot(grad_q, w_query, NT) + jnp.concatenate(
        [share_hidden, dot(grad_kc, w_key, NT) + dot(grad_vc, w_value, NT)], axis=0
    )
    grad_gain_one = jnp.sum(grad_hidden * norm_one, axis=0, keepdims=True)
    grad_input = grad_middle + norm_back(norm_one, scale_one, grad_hidden * gain_one)
    grad_input = jnp.concatenate(
        [
            grad_input[:prompt_rows]
            .reshape(NPR, PR_DEV, width)
            .transpose(1, 0, 2)
            .reshape(prompt_rows, width),
            grad_input[prompt_rows:],
        ],
        axis=0,
    )

    unit = 16 * dp * devices

    def summed(pieces):
        rows = jnp.concatenate(pieces, axis=0).astype(BF)
        count = rows.shape[0]
        rows = jnp.pad(rows, ((0, -count % unit), (0, 0)))
        return all_reduce(rows).astype(F32)

    first = summed([grad_out_proj, grad_router_t, grad_gain_two])
    last = summed([grad_query, grad_key, grad_value, grad_gain_one])
    return (
        outputs[None],
        grad_input[None],
        last[3 * width],
        last[:width],
        last[width : 2 * width],
        last[2 * width : 3 * width],
        first[:width],
        first[width + expert_count],
        first[width : width + expert_count].T,
        grad_w_in,
        grad_w_out,
    )


def solution(mesh):
    return jax.shard_map(
        per_device,
        mesh=mesh,
        in_specs=(
            P("dp", "expert", None),
            P(),
            P(),
            P(),
            P(),
            P(),
            P(),
            P(),
            P("expert", None, None),
            P("expert", None, None),
            P("dp", "expert", None),
            P("dp", "expert", None),
            P("dp", "expert"),
            P("dp", "expert", None),
        ),
        out_specs=(
            P("dp", "expert", None),
            P("dp", "expert", None),
            P(),
            P(),
            P(),
            P(),
            P(),
            P(),
            P(),
            P("expert", "dp", None),
            P("expert", "dp", None),
        ),
        check_vma=False,
    )
```

time: 960 us -> 756 us (0.79)
  waiting for transfers between devices: 533 us -> 286 us
  starting transfers between devices: 17.5 us -> 97.7 us
  local copies, waits for them, and re-layouts: 141 us -> 72.7 us
  Pallas kernels: 0 us -> 39 us
  matrix products: 140 us -> 172 us
  other arithmetic: 53.3 us -> 28.5 us
  between operations: 16.7 us -> 3.39 us
    reduce_scatter x2 -> x0, waiting for transfers between devices: 257 us -> none  [the longest x1 160 us: per_device(): lax.psum_scatter(grad_w_out.astype(jnp.bfloat16), 'dp', scatter_dimension...]
    ppermute x0 -> x42, waiting for transfers between devices: none -> 234 us  [swap(): return lax.ppermute(value, axis, [(i, i ^ mask) for i in range(size)])]
    psum x1 -> x0, waiting for transfers between devices: 196 us -> none  [per_device(): lax.psum((grad_query, grad_key, grad_value, grad_out_proj, grad_router, g...]
    ppermute x0 -> x42, starting transfers between devices: none -> 54.2 us  [swap(): return lax.ppermute(value, axis, [(i, i ^ mask) for i in range(size)])]
    all_gather x2 -> x0, waiting for transfers between devices: 47.5 us -> none  [the longest x1 24.5 us: per_device(): lax.all_gather(key_local, 'expert', axis=0, tiled=True)]
    all_to_all x0 -> x2, blocking collectives: none -> 47.3 us  [to_experts(): lax.all_to_all(slots, 'expert', split_axis=0, concat_axis=0, tiled=True)]
    psum x1 -> x0, blocking collectives: 47 us -> none  [per_device(): lax.psum((grad_query, grad_key, grad_value, grad_out_proj, grad_router, g...]
    all_to_all x4 -> x10, waiting for transfers between devices: 7.15 us -> 51.5 us  [the longest x9 51.5 us: to_experts(): lax.all_to_all(slots, 'expert', split_axis=0, concat_axis=0, tiled=True)]
  transfers between devices with their start and end apart: 10 -> 52, of which waited for: 7 -> 27; matrix products, arithmetic and copies ran while one was open for 19% -> 26% of each run, Pallas kernels for 0% -> 0%
where the time goes in v1:
time: 756 us; the launch traced here: 746 us
  waiting for transfers between devices  286 us (38%)
  matrix products  172 us (23%)
  starting transfers between devices  97.7 us (13%)
  local copies, waits for them, and re-layouts  72.7 us (10%)
  blocking collectives  47.3 us (6%)
  Pallas kernels  39 us (5%)
  other arithmetic  28.5 us (4%)
    ppermute x42, waiting for transfers between devices, swap(): return lax.ppermute(value, axis, [(i, i ^ mask) for i in range(size)])  234 us
    dot_general x45, matrix products, dot(): return lax.dot_general(a, b, (dims, ((), ())), preferred_element_type=out)  75.2 us
    ppermute x42, starting transfers between devices, swap(): return lax.ppermute(value, axis, [(i, i ^ mask) for i in range(size)])  54.2 us
    all_to_all x9, waiting for transfers between devices, to_experts(): lax.all_to_all(slots, 'expert', split_axis=0, concat_axis=0, tiled=True)  51.5 us
    all_to_all x2, blocking collectives, to_experts(): lax.all_to_all(slots, 'expert', split_axis=0, concat_axis=0, tiled=True)  47.3 us
    all_to_all x9, starting transfers between devices, to_experts(): lax.all_to_all(slots, 'expert', split_axis=0, concat_axis=0, tiled=True)  38.7 us
    pallas_call x1, Pallas kernels, attention_backward(): pl.pallas_call(attention_backward_kernel, grid_spec=pltpu.PrefetchScalarG...  22.6 us
    dot_general x1, matrix products, per_device(): jnp.einsum('erf,edf->erd', grad_pre, w_in, preferred_element_type=F32)  21.3 us
  transfers between devices with their start and end apart: 52, of which 27 were waited for; matrix products, arithmetic and copies ran while one was open for 26% of the time, Pallas kernels for 0%

profile of v1, /device:TPU:0, one launch (start us, length us, event | category | flops | bytes accessed | tf_op | source)
XLA Modules:
  0.0 746.1 jit_solution(6285240504519500005)
XLA Ops:
  7.9 9.3 %collective-permute-done.2 = bf16[256,768]{1,0:T(8,128)(2,1)S(1)} collective-permute-done((bf16[256,768]{1,0:T(8,128)(2,1)S(1)}, bf16[256,768]{1,0:T(8,128)(2,1)S(1)}, u32[]{:S(2)}, u32[]{:S(2)}) %collective-permute-start.2) | collective-permute-done | bytes 393248 | tf_op jit(solution)/shard_map/ppermute | solution.py:207
  17.3 7.5 %collective-permute-done.1 = bf16[256,768]{1,0:T(8,128)(2,1)S(1)} collective-permute-done((bf16[256,768]{1,0:T(8,128)(2,1)S(1)}, bf16[256,768]{1,0:T(8,128)(2,1)S(1)}, u32[]{:S(2)}, u32[]{:S(2)}) %collective-permute-start.1) | collective-permute-done | bytes 393248 | tf_op jit(solution)/shard_map/ppermute | solution.py:207
  42.1 16.4 %attention_forward.1 = (bf16[384,768]{1,0:T(8,128)(2,1)}, f32[6,3,256]{2,1,0:T(4,128)}) custom-call(s32[2]{0:T(128)} %pad_add_fusion.info, bf16[384,768]{1,0:T(8,128)(2,1)} %convolution_convert_fusion.14.q_ref, bf16[8,2,128,768]{3,2,1,0:T(8,128)(2,1)} %bitcast.379, bf16[8,2,128,768]{3,2,1,0:T(8,128)(2,1)} %bitcast.381, ...), custom_call_target="tpu_custom_call" | custom-call | flops 9663676416 | bytes 6291456 | tf_op jit(solution)/shard_map/attention_forward/pallas_call | solution.py:156
  61.6 23.9 %all_to_all.60 = bf16[8,128,768]{2,1,0:T(8,128)(2,1)S(1)} all-to-all(bf16[8,128,768]{2,1,0:T(8,128)(2,1)S(1)} %bitcast.367), channel_id=1, replica_groups=mesh['dp'=4,'expert'=8] {'expert'}, dimensions={0} | all-to-all | bytes 3145728 | tf_op jit(solution)/shard_map/all_to_all | solution.py:267
  86.8 12.2 %fusion.202 = f32[2,512,3072]{2,1,0:T(8,128)} fusion(bf16[2,512,768]{2,1,0:T(8,128)(2,1)S(1)} %bitcast.318, bf16[2,768,3072]{2,1,0:T(8,128)(2,1)} %param.22), kind=kOutput, calls=%fused_computation.403 | convolution fusion | flops 4831838208 | bytes 23592960 | tf_op jit(solution)/shard_map/erd,edf->erf/dot_general | solution.py:405
  99.1 10.3 %fusion.41 = bf16[2,512,768]{2,1,0:T(8,128)(2,1)S(1)} fusion(bf16[2,3072,768]{2,1,0:T(8,128)(2,1)S(1)} %bitcast.378, f32[2,512,3072]{2,1,0:T(8,128)} %fusion.202), kind=kOutput, calls=%fused_computation.70 | convolution fusion | flops 4860936192 | bytes 23592960 | tf_op jit(solution)/shard_map/erf,efd->erd/dot_general | solution.py:407
  109.5 23.4 %all_to_all.61 = bf16[8,128,768]{2,1,0:T(8,128)(2,1)S(1)} all-to-all(bf16[8,128,768]{2,1,0:T(8,128)(2,1)S(1)} %bitcast.327), channel_id=1, replica_groups=mesh['dp'=4,'expert'=8] {'expert'}, dimensions={0} | all-to-all | bytes 3145728 | tf_op jit(solution)/shard_map/all_to_all | solution.py:267
  142.7 13.6 %collective-permute-done.6 = bf16[400,768]{1,0:T(8,128)(2,1)S(1)} collective-permute-done((bf16[400,768]{1,0:T(8,128)(2,1)S(1)}, bf16[400,768]{1,0:T(8,128)(2,1)S(1)}, u32[]{:S(2)}, u32[]{:S(2)}) %collective-permute-start.6) | collective-permute-done | bytes 614432 | tf_op jit(solution)/shard_map/ppermute | solution.py:207
  157.2 36.0 %collective-permute-done.5 = bf16[400,768]{1,0:T(8,128)(2,1)S(1)} collective-permute-done((bf16[400,768]{1,0:T(8,128)(2,1)S(1)}, bf16[400,768]{1,0:T(8,128)(2,1)S(1)}, u32[]{:S(2)}, u32[]{:S(2)}) %collective-permute-start.5) | collective-permute-done | bytes 614432 | tf_op jit(solution)/shard_map/ppermute | solution.py:207
  210.0 28.6 %collective-permute-done.40 = bf16[384,768]{1,0:T(8,128)(2,1)} collective-permute-done((bf16[384,768]{1,0:T(8,128)(2,1)S(1)}, bf16[384,768]{1,0:T(8,128)(2,1)}, u32[]{:S(2)}, u32[]{:S(2)}) %collective-permute-start.40) | collective-permute-done | bytes 589856 | tf_op jit(solution)/shard_map/ppermute | solution.py:207
  250.3 14.2 %collective-permute-done.41 = bf16[384,768]{1,0:T(8,128)(2,1)S(1)} collective-permute-done((bf16[384,768]{1,0:T(8,128)(2,1)S(1)}, bf16[384,768]{1,0:T(8,128)(2,1)S(1)}, u32[]{:S(2)}, u32[]{:S(2)}) %collective-permute-start.41) | collective-permute-done | bytes 589856 | tf_op jit(solution)/shard_map/ppermute | solution.py:207
  280.3 12.6 %all-to-all-done.7 = bf16[8,128,768]{2,1,0:T(8,128)(2,1)} async-done(((bf16[8,128,768]{2,1,0:T(8,128)(2,1)}), bf16[8,128,768]{2,1,0:T(8,128)(2,1)}, u32[]{:S(2)}, u32[]{:S(2)}) %all-to-all-start.7) | async-done | bytes 1572896 | tf_op jit(solution)/shard_map/all_to_all | solution.py:267
  311.1 7.1 all-to-all-done.5
  329.8 13.8 %all-to-all-done.10 = bf16[8,128,768]{2,1,0:T(8,128)(2,1)} async-done(((bf16[8,128,768]{2,1,0:T(8,128)(2,1)}), bf16[8,128,768]{2,1,0:T(8,128)(2,1)}, u32[]{:S(2)}, u32[]{:S(2)}) %all-to-all-start.10) | async-done | bytes 1572896 | tf_op jit(solution)/shard_map/all_to_all | solution.py:267
  353.3 15.7 %all-to-all-done.9 = bf16[8,128,768]{2,1,0:T(8,128)(2,1)} async-done(((bf16[8,128,768]{2,1,0:T(8,128)(2,1)}), bf16[8,128,768]{2,1,0:T(8,128)(2,1)}, u32[]{:S(2)}, u32[]{:S(2)}) %all-to-all-start.9) | async-done | bytes 1572896 | tf_op jit(solution)/shard_map/all_to_all | solution.py:267
  373.5 21.3 %fusion.40 = bf16[2,512,768]{2,1,0:T(8,128)(2,1)} fusion(bf16[2,768,3072]{2,1,0:T(8,128)(2,1)} %param.22, f32[2,512,3072]{2,1,0:T(8,128)} %fusion.202, bf16[2,3072,768]{2,1,0:T(8,128)(2,1)} %param.23, bf16[1,512,768]{2,1,0:T(8,128)(2,1)S(1)} %copy-done.35, bf16[1,512,768]{2,1,0:T(8,128)(2,1)} %fusion.58), kind=kOutput, calls=%fused_computation.69 | convolution fusion | flops 9725018112 | bytes 34603008 | tf_op jit(solution)/shard_map/erf,edf->erd/dot_general | solution.py:418
  421.9 13.2 %fusion.33 = f32[2,2048,768]{2,1,0:T(8,128)} fusion(bf16[2,768,3072]{2,1,0:T(8,128)(2,1)} %param.22, s32[]{:T(128)S(6)} %select_n.268, bf16[2,512,768]{2,1,0:T(8,128)(2,1)} %bitcast.355, bf16[2,512,768]{2,1,0:T(8,128)(2,1)} %bitcast.357, bf16[2,512,768]{2,1,0:T(8,128)(2,1)} %bitcast.359, bf16[2,512,768]{2,1,0:T(8,128)(2,1)} %bitcast.320), kind=kOutput, calls=%fused_computation.51 | convolution fusion | flops 4857004032 | bytes 21233668 | tf_op jit(solution)/shard_map/erd,edf->erf/dot_general | solution.py:431
  435.1 11.8 %fusion.35 = f32[2,2048,768]{2,1,0:T(8,128)} fusion(bf16[2,3072,768]{2,1,0:T(8,128)(2,1)} %param.23, s32[]{:T(128)S(6)} %select_n.268, bf16[1,512,768]{2,1,0:T(8,128)(2,1)} %fusion.50, bf16[1,512,768]{2,1,0:T(8,128)(2,1)} %fusion.51, bf16[1,512,768]{2,1,0:T(8,128)(2,1)} %fusion.52, bf16[1,512,768]{2,1,0:T(8,128)(2,1)} %fusion.53, ...), kind=kOutput, calls=%fused_computation.53 | convolution fusion | flops 4882169856 | bytes 21233668 | tf_op jit(solution)/shard_map/erd,efd->erf/dot_general | solution.py:433
  446.9 17.6 %fusion.37 = bf16[2,768,768]{2,1,0:T(8,128)(2,1)} fusion(f32[2,2048,768]{2,1,0:T(8,128)} %fusion.35, f32[2,2048,768]{2,1,0:T(8,128)} %fusion.33, bf16[2,512,768]{2,1,0:T(8,128)(2,1)} %bitcast.356, bf16[2,512,768]{2,1,0:T(8,128)(2,1)} %bitcast.358, bf16[2,512,768]{2,1,0:T(8,128)(2,1)} %bitcast.360, bf16[2,512,768]{2,1,0:T(8,128)(2,1)} %bitcast.321), kind=kOutput, calls=%fused_computation.57 | convolution fusion | flops 4917952512 | bytes 33816576 | tf_op jit(solution)/shard_map/erd,erf->edf/dot_general | solution.py:435
  471.4 22.6 %attention_backward.1 = (bf16[384,768]{1,0:T(8,128)(2,1)}, bf16[8,2,128,768]{3,2,1,0:T(8,128)(2,1)}, bf16[8,2,128,768]{3,2,1,0:T(8,128)(2,1)}, bf16[128,768]{1,0:T(8,128)(2,1)}, bf16[128,768]{1,0:T(8,128)(2,1)}) custom-call(s32[2]{0:T(128)} %pad_add_fusion.info, bf16[384,768]{1,0:T(8,128)(2,1)} %convolution_convert_fusion.14.q_ref, ...), custom_call_target="tpu_custom_call" | custom-call | flops 24159191040 | bytes 12582912 | tf_op jit(solution)/shard_map/attention_backward/pallas_call | solution.py:179
  494.0 4.8 fusion.205
  516.7 4.6 collective-permute-done.28
  526.7 8.1 %collective-permute-start.30 = (bf16[32,768]{1,0:T(8,128)(2,1)S(1)}, bf16[32,768]{1,0:T(8,128)(2,1)S(1)}, u32[]{:S(2)}, u32[]{:S(2)}) collective-permute-start(bf16[32,768]{1,0:T(8,128)(2,1)S(1)} %get-tuple-element.122), channel_id=1, source_target_pairs={{0,16},{8,24},{16,0},{24,8},{1,17},{9,25},{17,1},{25,9},{2,18},{10... | collective-permute-start | bytes 147464 | tf_op jit(solution)/shard_map/ppermute | solution.py:207
  542.3 6.3 collective-permute-done.10
  548.6 6.5 collective-permute-done.9
  562.4 10.3 %fusion.21 = f32[2,768,768]{2,1,0:T(8,128)} fusion(f32[2,2048,768]{2,1,0:T(8,128)S(1)} %bitcast.384, bf16[1,512,768]{2,1,0:T(8,128)(2,1)S(1)} %copy-done.39, bf16[1,512,768]{2,1,0:T(8,128)(2,1)S(1)} %copy-done.40, bf16[1,512,768]{2,1,0:T(8,128)(2,1)S(1)} %copy-done.41, bf16[1,512,768]{2,1,0:T(8,128)(2,1)S(1)} %copy-done.42, ...), kind=kOutput, calls=%fused_computation.31 | convolution fusion | flops 4910481408 | bytes 23592960 | tf_op jit(solution)/shard_map/erf,erd->efd/dot_general | solution.py:436
  574.2 4.8 all-to-all-start.11
  584.8 51.8 %collective-permute-done.33 = bf16[32,768]{1,0:T(8,128)(2,1)S(1)} collective-permute-done((bf16[32,768]{1,0:T(8,128)(2,1)}, bf16[32,768]{1,0:T(8,128)(2,1)S(1)}, u32[]{:S(2)}, u32[]{:S(2)}) %collective-permute-start.33) | collective-permute-done | bytes 49184 | tf_op jit(solution)/shard_map/ppermute | solution.py:207
  647.1 20.8 %collective-permute-done.35 = bf16[4,32,768]{2,1,0:T(8,128)(2,1)S(1)} collective-permute-done((bf16[4,32,768]{2,1,0:T(8,128)(2,1)S(1)}, bf16[4,32,768]{2,1,0:T(8,128)(2,1)S(1)}, u32[]{:S(2)}, u32[]{:S(2)}) %collective-permute-start.35) | collective-permute-done | bytes 196640 | tf_op jit(solution)/shard_map/ppermute | solution.py:207
  688.2 6.7 collective-permute-done.19
  704.1 5.1 collective-permute-done.21
  710.0 11.4 %collective-permute-done.22 = bf16[4,80,768]{2,1,0:T(8,128)(2,1)S(1)} collective-permute-done((bf16[4,80,768]{2,1,0:T(8,128)(2,1)S(1)}, bf16[4,80,768]{2,1,0:T(8,128)(2,1)S(1)}, u32[]{:S(2)}, u32[]{:S(2)}) %collective-permute-start.22) | collective-permute-done | bytes 491552 | tf_op jit(solution)/shard_map/ppermute | solution.py:207
  (459 shorter events, 270.3 us)
Async XLA Ops:
  7.3 17.5 %collective-permute-start.1 = (bf16[256,768]{1,0:T(8,128)(2,1)S(1)}, bf16[256,768]{1,0:T(8,128)(2,1)S(1)}, u32[]{:S(2)}, u32[]{:S(2)}) collective-permute-start(bf16[256,768]{1,0:T(8,128)(2,1)S(1)} %get-tuple-element.116), channel_id=1, source_target_pairs={{0,4},{1,5},{2,6},{3,7},{4,0},{5,1},{6,2},{7,3},{8,12},{9,13},{10,... | collective-permute-start | bytes 1179656 | tf_op jit(solution)/shard_map/ppermute | solution.py:207
  7.8 17.3 %collective-permute-start = (bf16[256,768]{1,0:T(8,128)(2,1)S(1)}, bf16[256,768]{1,0:T(8,128)(2,1)S(1)}, u32[]{:S(2)}, u32[]{:S(2)}) collective-permute-start(bf16[256,768]{1,0:T(8,128)(2,1)S(1)} %get-tuple-element.116), channel_id=1, source_target_pairs={{0,2},{1,3},{2,0},{3,1},{4,6},{5,7},{6,4},{7,5},{8,10},{9,11},{10,... | collective-permute-start | bytes 1179656 | tf_op jit(solution)/shard_map/ppermute | solution.py:207
  137.5 18.8 %collective-permute-start.6 = (bf16[400,768]{1,0:T(8,128)(2,1)S(1)}, bf16[400,768]{1,0:T(8,128)(2,1)S(1)}, u32[]{:S(2)}, u32[]{:S(2)}) collective-permute-start(bf16[400,768]{1,0:T(8,128)(2,1)S(1)} %fusion.109), channel_id=1, source_target_pairs={{0,24},{8,16},{16,8},{24,0},{1,25},{9,17},{17,9},{25,1},{2,26},{10... | collective-permute-start | bytes 1843208 | tf_op jit(solution)/shard_map/ppermute | solution.py:207
  141.3 51.8 %collective-permute-start.5 = (bf16[400,768]{1,0:T(8,128)(2,1)S(1)}, bf16[400,768]{1,0:T(8,128)(2,1)S(1)}, u32[]{:S(2)}, u32[]{:S(2)}) collective-permute-start(bf16[400,768]{1,0:T(8,128)(2,1)S(1)} %fusion.109), channel_id=1, source_target_pairs={{0,16},{8,24},{16,0},{24,8},{1,17},{9,25},{17,1},{25,9},{2,18},{10... | collective-permute-start | bytes 1843208 | tf_op jit(solution)/shard_map/ppermute | solution.py:207
  141.9 51.3 %collective-permute-start.4 = (bf16[400,768]{1,0:T(8,128)(2,1)S(1)}, bf16[400,768]{1,0:T(8,128)(2,1)S(1)}, u32[]{:S(2)}, u32[]{:S(2)}) collective-permute-start(bf16[400,768]{1,0:T(8,128)(2,1)S(1)} %fusion.109), channel_id=1, source_target_pairs={{0,8},{8,0},{16,24},{24,16},{1,9},{9,1},{17,25},{25,17},{2,10},{10... | collective-permute-start | bytes 1843208 | tf_op jit(solution)/shard_map/ppermute | solution.py:207
  205.2 36.7 %all-to-all-start.3 = ((bf16[8,128,768]{2,1,0:T(8,128)(2,1)}), bf16[8,128,768]{2,1,0:T(8,128)(2,1)}, u32[]{:S(2)}, u32[]{:S(2)}) async-start(bf16[8,128,768]{2,1,0:T(8,128)(2,1)} %bitcast.352), calls=%async_computation.3 | async-start | bytes 3145728 | tf_op jit(solution)/shard_map/all_to_all | solution.py:267
  209.5 29.1 %collective-permute-start.40 = (bf16[384,768]{1,0:T(8,128)(2,1)S(1)}, bf16[384,768]{1,0:T(8,128)(2,1)}, u32[]{:S(2)}, u32[]{:S(2)}) collective-permute-start(bf16[384,768]{1,0:T(8,128)(2,1)S(1)} %multiply_convert_fusion.6), channel_id=1, source_target_pairs={{0,16},{8,24},{16,0},{24,8},{1,17},{9,25},{17,1},{25,9},{2,18},{10... | collective-permute-start | bytes 1769480 | tf_op jit(solution)/shard_map/ppermute | solution.py:207
  241.9 25.5 %all-to-all-start.6 = ((bf16[8,128,768]{2,1,0:T(8,128)(2,1)}), bf16[8,128,768]{2,1,0:T(8,128)(2,1)}, u32[]{:S(2)}, u32[]{:S(2)}) async-start(bf16[8,128,768]{2,1,0:T(8,128)(2,1)} %bitcast.362), calls=%async_computation.6 | async-start | bytes 3145728 | tf_op jit(solution)/shard_map/all_to_all | solution.py:267
  246.4 18.1 %collective-permute-start.41 = (bf16[384,768]{1,0:T(8,128)(2,1)S(1)}, bf16[384,768]{1,0:T(8,128)(2,1)S(1)}, u32[]{:S(2)}, u32[]{:S(2)}) collective-permute-start(bf16[384,768]{1,0:T(8,128)(2,1)S(1)} %multiply_convert_fusion.6), channel_id=1, source_target_pairs={{0,24},{8,16},{16,8},{24,0},{1,25},{9,17},{17,9},{25,1},{2,26},{10... | collective-permute-start | bytes 1769480 | tf_op jit(solution)/shard_map/ppermute | solution.py:207
  247.8 29.2 %collective-permute-start.39 = (bf16[384,768]{1,0:T(8,128)(2,1)S(1)}, bf16[384,768]{1,0:T(8,128)(2,1)}, u32[]{:S(2)}, u32[]{:S(2)}) collective-permute-start(bf16[384,768]{1,0:T(8,128)(2,1)S(1)} %multiply_convert_fusion.6), channel_id=1, source_target_pairs={{0,8},{8,0},{16,24},{24,16},{1,9},{9,1},{17,25},{25,17},{2,10},{10... | collective-permute-start | bytes 1769480 | tf_op jit(solution)/shard_map/ppermute | solution.py:207
  267.4 25.5 %all-to-all-start.7 = ((bf16[8,128,768]{2,1,0:T(8,128)(2,1)}), bf16[8,128,768]{2,1,0:T(8,128)(2,1)}, u32[]{:S(2)}, u32[]{:S(2)}) async-start(bf16[8,128,768]{2,1,0:T(8,128)(2,1)} %bitcast.363), calls=%async_computation.7 | async-start | bytes 3145728 | tf_op jit(solution)/shard_map/all_to_all | solution.py:267
  292.9 25.3 %all-to-all-start.5 = ((bf16[8,128,768]{2,1,0:T(8,128)(2,1)}), bf16[8,128,768]{2,1,0:T(8,128)(2,1)}, u32[]{:S(2)}, u32[]{:S(2)}) async-start(bf16[8,128,768]{2,1,0:T(8,128)(2,1)} %bitcast.361), calls=%async_computation.5 | async-start | bytes 3145728 | tf_op jit(solution)/shard_map/all_to_all | solution.py:267
  318.2 25.3 %all-to-all-start.10 = ((bf16[8,128,768]{2,1,0:T(8,128)(2,1)}), bf16[8,128,768]{2,1,0:T(8,128)(2,1)}, u32[]{:S(2)}, u32[]{:S(2)}) async-start(bf16[8,128,768]{2,1,0:T(8,128)(2,1)} %bitcast.354), calls=%async_computation.10 | async-start | bytes 3145728 | tf_op jit(solution)/shard_map/all_to_all | solution.py:267
  343.5 25.5 %all-to-all-start.9 = ((bf16[8,128,768]{2,1,0:T(8,128)(2,1)}), bf16[8,128,768]{2,1,0:T(8,128)(2,1)}, u32[]{:S(2)}, u32[]{:S(2)}) async-start(bf16[8,128,768]{2,1,0:T(8,128)(2,1)} %bitcast.353), calls=%async_computation.9 | async-start | bytes 3145728 | tf_op jit(solution)/shard_map/all_to_all | solution.py:267
  369.1 40.3 %all-to-all-start.8 = ((bf16[8,128,768]{2,1,0:T(8,128)(2,1)}), bf16[8,128,768]{2,1,0:T(8,128)(2,1)}, u32[]{:S(2)}, u32[]{:S(2)}) async-start(bf16[8,128,768]{2,1,0:T(8,128)(2,1)} %bitcast.351), calls=%async_computation.8 | async-start | bytes 3145728 | tf_op jit(solution)/shard_map/all_to_all | solution.py:267
  409.4 55.1 %all-to-all-start.4 = ((bf16[8,128,768]{2,1,0:T(8,128)(2,1)}), bf16[8,128,768]{2,1,0:T(8,128)(2,1)}, u32[]{:S(2)}, u32[]{:S(2)}) async-start(bf16[8,128,768]{2,1,0:T(8,128)(2,1)} %bitcast.322), calls=%async_computation.4 | async-start | bytes 3145728 | tf_op jit(solution)/shard_map/all_to_all | solution.py:267
  502.0 33.0 %collective-permute-start.7 = (bf16[4,256,768]{2,1,0:T(8,128)(2,1)S(1)}, bf16[4,256,768]{2,1,0:T(8,128)(2,1)S(1)}, u32[]{:S(2)}, u32[]{:S(2)}) collective-permute-start(bf16[4,256,768]{2,1,0:T(8,128)(2,1)S(1)} %slice_bitcast_fusion), channel_id=1, source_target_pairs={{0,1},{1,0},{2,3},{3,2},{4,5},{5,4},{6,7},{7,6},{8,9},{9,8},{10,11... | collective-permute-start | bytes 4718600 | tf_op jit(solution)/shard_map/ppermute | solution.py:207
  537.1 18.0 %collective-permute-start.9 = (bf16[256,768]{1,0:T(8,128)(2,1)S(1)}, bf16[256,768]{1,0:T(8,128)(2,1)S(1)}, u32[]{:S(2)}, u32[]{:S(2)}) collective-permute-start(bf16[256,768]{1,0:T(8,128)(2,1)S(1)} %get-tuple-element.102), channel_id=1, source_target_pairs={{0,4},{1,5},{2,6},{3,7},{4,0},{5,1},{6,2},{7,3},{8,12},{9,13},{10,... | collective-permute-start | bytes 1179656 | tf_op jit(solution)/shard_map/ppermute | solution.py:207
  538.5 16.9 %collective-permute-start.8 = (bf16[256,768]{1,0:T(8,128)(2,1)S(1)}, bf16[256,768]{1,0:T(8,128)(2,1)S(1)}, u32[]{:S(2)}, u32[]{:S(2)}) collective-permute-start(bf16[256,768]{1,0:T(8,128)(2,1)S(1)} %get-tuple-element.100), channel_id=1, source_target_pairs={{0,2},{1,3},{2,0},{3,1},{4,6},{5,7},{6,4},{7,5},{8,10},{9,11},{10,... | collective-permute-start | bytes 1179656 | tf_op jit(solution)/shard_map/ppermute | solution.py:207
  540.4 43.1 %collective-permute-start.32 = (bf16[32,768]{1,0:T(8,128)(2,1)}, bf16[32,768]{1,0:T(8,128)(2,1)}, u32[]{:S(2)}, u32[]{:S(2)}) collective-permute-start(bf16[32,768]{1,0:T(8,128)(2,1)} %get-tuple-element.76), channel_id=1, source_target_pairs={{0,8},{8,0},{16,24},{24,16},{1,9},{9,1},{17,25},{25,17},{2,10},{10... | collective-permute-start | bytes 147464 | tf_op jit(solution)/shard_map/ppermute | solution.py:207
  561.1 76.2 %collective-permute-start.11 = (bf16[4,4,80,768]{3,2,1,0:T(8,128)(2,1)}, bf16[4,4,80,768]{3,2,1,0:T(8,128)(2,1)}, u32[]{:S(2)}, u32[]{:S(2)}) collective-permute-start(bf16[4,4,80,768]{3,2,1,0:T(8,128)(2,1)} %dynamic-slice_bitcast_fusion), channel_id=1, source_target_pairs={{0,1},{1,0},{2,3},{3,2},{4,5},{5,4},{6,7},{7,6},{8,9},{9,8},{10,11... | collective-permute-start | bytes 5898248 | tf_op jit(solution)/shard_map/ppermute | solution.py:207
  574.2 158.1 %all-to-all-start.11 = ((bf16[4,2,192,768]{3,2,1,0:T(8,128)(2,1)}), bf16[4,2,192,768]{3,2,1,0:T(8,128)(2,1)}, u32[]{:S(2)}, u32[]{:S(2)}) async-start(bf16[4,2,192,768]{3,2,1,0:T(8,128)(2,1)} %bitcast.317), calls=%async_computation.11 | async-start | bytes 4718592 | tf_op jit(solution)/shard_map/all_to_all | solution.py:441
  579.0 57.7 %collective-permute-start.33 = (bf16[32,768]{1,0:T(8,128)(2,1)}, bf16[32,768]{1,0:T(8,128)(2,1)S(1)}, u32[]{:S(2)}, u32[]{:S(2)}) collective-permute-start(bf16[32,768]{1,0:T(8,128)(2,1)} %get-tuple-element.76), channel_id=1, source_target_pairs={{0,16},{8,24},{16,0},{24,8},{1,17},{9,25},{17,1},{25,9},{2,18},{10... | collective-permute-start | bytes 147464 | tf_op jit(solution)/shard_map/ppermute | solution.py:207
  582.0 61.6 %collective-permute-start.34 = (bf16[32,768]{1,0:T(8,128)(2,1)}, bf16[32,768]{1,0:T(8,128)(2,1)S(1)}, u32[]{:S(2)}, u32[]{:S(2)}) collective-permute-start(bf16[32,768]{1,0:T(8,128)(2,1)} %get-tuple-element.76), channel_id=1, source_target_pairs={{0,24},{8,16},{16,8},{24,0},{1,25},{9,17},{17,9},{25,1},{2,26},{10... | collective-permute-start | bytes 147464 | tf_op jit(solution)/shard_map/ppermute | solution.py:207
  640.0 30.3 %collective-permute-start.14 = (bf16[4,80,768]{2,1,0:T(8,128)(2,1)S(1)}, bf16[4,80,768]{2,1,0:T(8,128)(2,1)S(1)}, u32[]{:S(2)}, u32[]{:S(2)}) collective-permute-start(bf16[4,80,768]{2,1,0:T(8,128)(2,1)S(1)} %get-tuple-element.86), channel_id=1, source_target_pairs={{0,6},{1,7},{2,4},{3,5},{4,2},{5,3},{6,0},{7,1},{8,14},{9,15},{10,... | collective-permute-start | bytes 1474568 | tf_op jit(solution)/shard_map/ppermute | solution.py:207
  641.1 29.2 %collective-permute-start.13 = (bf16[4,80,768]{2,1,0:T(8,128)(2,1)S(1)}, bf16[4,80,768]{2,1,0:T(8,128)(2,1)S(1)}, u32[]{:S(2)}, u32[]{:S(2)}) collective-permute-start(bf16[4,80,768]{2,1,0:T(8,128)(2,1)S(1)} %get-tuple-element.87), channel_id=1, source_target_pairs={{0,4},{1,5},{2,6},{3,7},{4,0},{5,1},{6,2},{7,3},{8,12},{9,13},{10,... | collective-permute-start | bytes 1474568 | tf_op jit(solution)/shard_map/ppermute | solution.py:207
  643.2 27.1 %collective-permute-start.12 = (bf16[4,80,768]{2,1,0:T(8,128)(2,1)S(1)}, bf16[4,80,768]{2,1,0:T(8,128)(2,1)S(1)}, u32[]{:S(2)}, u32[]{:S(2)}) collective-permute-start(bf16[4,80,768]{2,1,0:T(8,128)(2,1)S(1)} %get-tuple-element.85), channel_id=1, source_target_pairs={{0,2},{1,3},{2,0},{3,1},{4,6},{5,7},{6,4},{7,5},{8,10},{9,11},{10,... | collective-permute-start | bytes 1474568 | tf_op jit(solution)/shard_map/ppermute | solution.py:207
  643.6 24.3 %collective-permute-start.35 = (bf16[4,32,768]{2,1,0:T(8,128)(2,1)S(1)}, bf16[4,32,768]{2,1,0:T(8,128)(2,1)S(1)}, u32[]{:S(2)}, u32[]{:S(2)}) collective-permute-start(bf16[4,32,768]{2,1,0:T(8,128)(2,1)S(1)} %bitcast_dynamic-update-slice_fusion.16), channel_id=1, source_target_pairs={{0,2},{1,3},{2,0},{3,1},{4,6},{5,7},{6,4},{7,5},{8,10},{9,11},{10,... | collective-permute-start | bytes 589832 | tf_op jit(solution)/shard_map/ppermute | solution.py:207
  645.3 29.8 %collective-permute-start.36 = (bf16[4,32,768]{2,1,0:T(8,128)(2,1)S(1)}, bf16[4,32,768]{2,1,0:T(8,128)(2,1)S(1)}, u32[]{:S(2)}, u32[]{:S(2)}) collective-permute-start(bf16[4,32,768]{2,1,0:T(8,128)(2,1)S(1)} %bitcast_dynamic-update-slice_fusion.16), channel_id=1, source_target_pairs={{0,4},{1,5},{2,6},{3,7},{4,0},{5,1},{6,2},{7,3},{8,12},{9,13},{10,... | collective-permute-start | bytes 589832 | tf_op jit(solution)/shard_map/ppermute | solution.py:207
  682.5 43.3 %collective-permute-start.38 = (bf16[4,4,32,768]{3,2,1,0:T(8,128)(2,1)}, bf16[4,4,32,768]{3,2,1,0:T(8,128)(2,1)}, u32[]{:S(2)}, u32[]{:S(2)}) collective-permute-start(bf16[4,4,32,768]{3,2,1,0:T(8,128)(2,1)} %bitcast_dynamic-update-slice_fusion.8), channel_id=1, source_target_pairs={{0,1},{1,0},{2,3},{3,2},{4,5},{5,4},{6,7},{7,6},{8,9},{9,8},{10,11... | collective-permute-start | bytes 2359304 | tf_op jit(solution)/shard_map/ppermute | solution.py:207
  698.4 23.0 %collective-permute-start.22 = (bf16[4,80,768]{2,1,0:T(8,128)(2,1)S(1)}, bf16[4,80,768]{2,1,0:T(8,128)(2,1)S(1)}, u32[]{:S(2)}, u32[]{:S(2)}) collective-permute-start(bf16[4,80,768]{2,1,0:T(8,128)(2,1)S(1)} %bitcast_dynamic-update-slice_fusion.12), channel_id=1, source_target_pairs={{0,4},{1,5},{2,6},{3,7},{4,0},{5,1},{6,2},{7,3},{8,12},{9,13},{10,... | collective-permute-start | bytes 1474568 | tf_op jit(solution)/shard_map/ppermute | solution.py:207
  700.4 21.8 %collective-permute-start.23 = (bf16[4,80,768]{2,1,0:T(8,128)(2,1)S(1)}, bf16[4,80,768]{2,1,0:T(8,128)(2,1)S(1)}, u32[]{:S(2)}, u32[]{:S(2)}) collective-permute-start(bf16[4,80,768]{2,1,0:T(8,128)(2,1)S(1)} %bitcast_dynamic-update-slice_fusion.12), channel_id=1, source_target_pairs={{0,6},{1,7},{2,4},{3,5},{4,2},{5,3},{6,0},{7,1},{8,14},{9,15},{10,... | collective-permute-start | bytes 1474568 | tf_op jit(solution)/shard_map/ppermute | solution.py:207
  (118 other events, 1411.7 us)

commit v2 on v1

v2 whole, which is shorter than its diff:
```python
import jax
import jax.numpy as jnp
from jax import lax
from jax.experimental import pallas as pl
from jax.experimental.pallas import tpu as pltpu
from jax.sharding import PartitionSpec as P

H = 12
HD = 64
TOP = 2
NPR = 2
CLEN = 128
PR_DEV = 128
PAIR = 2 * HD
TWO = 2 * PR_DEV

NEGATIVE = -1e30
BF = jnp.bfloat16
F32 = jnp.float32
SCALE = HD ** (-0.5)
MIB = 1024 * 1024

NN = ((1,), (0,))
NT = ((1,), (1,))
TN = ((0,), (0,))

HIGH, LOW, ROUTE = 0, 2, 4
TABLE = 16


def dot(a, b, dims=NN):
    return lax.dot_general(a, b, (dims, ((), ())), preferred_element_type=F32)


def iota(shape, dim):
    return lax.broadcasted_iota(jnp.int32, shape, dim)


def shape_of(shape, dtype):
    return jax.ShapeDtypeStruct(shape, dtype)


WEIGHT = 1.0
TIMES = {
    "norm": 2.7,
    "table": 4.5,
    "attention_forward": 15.0,
    "middle": 5.1,
    "dispatch_cot": 7.0,
    "expert_forward": 20.0,
    "expert_backward": 20.0,
    "dispatch": 6.5,
    "expert_weights": 9.0,
    "combine": 9.6,
    "attention_backward": 15.0,
    "sum_cores": 4.0,
    "halves": 3.1,
    "expert_weights_last": 30.0,
    "sum_chips": 2.6,
    "sum_groups": 1.8,
    "input": 1.0,
    "spread_sums": 9.0,
    "columns": 4.1,
}


def cost(name):
    flops = int(TIMES[name] * WEIGHT * 1.1e9)
    return pl.CostEstimate(flops=flops, bytes_accessed=0, transcendentals=0)


def run(kernel, name, info, operands, outs, deps=(), scratch=()):
    n_in, n_dep, n_out = len(operands), len(deps), len(outs)

    def body(info_ref, *refs):
        ins = refs[:n_in]
        results = refs[n_in + n_dep : n_in + n_dep + n_out]
        kernel(info_ref, ins, results, refs[n_in + n_dep + n_out :])

    vmem = pl.BlockSpec(memory_space=pltpu.VMEM)
    return pl.pallas_call(
        body,
        in_specs=[pl.BlockSpec(memory_space=pltpu.SMEM)]
        + [vmem] * n_in
        + [pl.BlockSpec(memory_space=pl.ANY)] * n_dep,
        out_specs=[vmem] * n_out,
        out_shape=list(outs),
        scratch_shapes=list(scratch),
        compiler_params=pltpu.CompilerParams(vmem_limit_bytes=56 * MIB),
        cost_estimate=cost(name),
        name=name,
    )(info, *operands, *deps)


def fill_bias(bias_ref, device, chips):
    for b in range(2 * chips):
        mask = 2 * (b % chips) + b // chips
        offset = (jnp.bitwise_xor(device, mask) - device) * PR_DEV
        seen = iota((PR_DEV, PR_DEV), 0) + offset <= iota((PR_DEV, PR_DEV), 1)
        bias_ref[b * PR_DEV : (b + 1) * PR_DEV, :] = jnp.where(seen, 0.0, NEGATIVE)


def two_heads(rows):
    keep = (iota((TWO, PAIR), 0) < PR_DEV) == (iota((TWO, PAIR), 1) < HD)
    return jnp.where(keep, jnp.concatenate([rows, rows], axis=0), jnp.zeros((), rows.dtype))


def join_heads(both):
    first = iota((PAIR, PR_DEV), 0) < HD
    return jnp.where(first, both[:, :PR_DEV], both[:, PR_DEV:]).T


def twice(block):
    return jnp.concatenate([block, block], axis=1)


def top_of(parts):
    top = jnp.max(parts[0], axis=0, keepdims=True)
    for part in parts[1:]:
        top = jnp.maximum(top, jnp.max(part, axis=0, keepdims=True))
    return top


def sum_of(parts):
    total = jnp.sum(parts[0], axis=0, keepdims=True)
    for part in parts[1:]:
        total = total + jnp.sum(part, axis=0, keepdims=True)
    return total


def added(parts):
    total = parts[0]
    for part in parts[1:]:
        total = total + part
    return total


def scores_of(keys, q2, bias_ref, group, span):
    parts = []
    for i, k in enumerate(keys):
        st = dot(k, q2, NT)
        if group < NPR:
            st = st + twice(bias_ref[i * span : (i + 1) * span, :])
        elif i == 2:
            st = st + twice(bias_ref[:PR_DEV, :])
        parts.append(st)
    return parts


def attention_forward_kernel(
    info, q_ref, ka_ref, kb_ref, va_ref, vb_ref, kc_ref, vc_ref, o_ref, lse_ref, bias_ref
):
    chips = ka_ref.shape[0]
    span = chips * PR_DEV
    device, chosen = info[0], info[1]

    @pl.when(pl.program_id(0) == 0)
    def _():
        fill_bias(bias_ref, device, chips)

    for group in range(3):
        rows = slice(group * PR_DEV, (group + 1) * PR_DEV)
        q2 = two_heads(q_ref[rows, :] * jnp.asarray(SCALE, BF))
        which = group if group < NPR else chosen
        keys = [ref[:, which].reshape(span, PAIR) for ref in (ka_ref, kb_ref)]
        values = [ref[:, which].reshape(span, PAIR) for ref in (va_ref, vb_ref)]
        if group == NPR:
            keys.append(kc_ref[...])
            values.append(vc_ref[...])
        scores = scores_of(keys, q2, bias_ref, group, span)
        top = top_of(scores)
        probs = [jnp.exp(st - top) for st in scores]
        total = sum_of(probs)
        both = added([dot(v, p.astype(BF), TN) for v, p in zip(values, probs)])
        both = both * (1.0 / total)
        o_ref[rows, :] = join_heads(both).astype(BF)
        lse_ref[0, group : group + 1, :] = top + jnp.log(total)


def attention_backward_kernel(
    info, q_ref, ka_ref, kb_ref, va_ref, vb_ref, kc_ref, vc_ref, do_ref, lse_ref,
    dq_ref, dka_ref, dkb_ref, dva_ref, dvb_ref, dkc_ref, dvc_ref, bias_ref, dk_acc, dv_acc,
):
    chips = ka_ref.shape[0]
    span = chips * PR_DEV
    device, chosen = info[0], info[1]

    @pl.when(pl.program_id(0) == 0)
    def _():
        fill_bias(bias_ref, device, chips)

    for group in range(3):
        rows = slice(group * PR_DEV, (group + 1) * PR_DEV)
        q2 = two_heads(q_ref[rows, :] * jnp.asarray(SCALE, BF))
        do2 = two_heads(do_ref[rows, :])
        lse = lse_ref[0, group : group + 1, :]
        which = group if group < NPR else chosen
        keys = [ref[:, which].reshape(span, PAIR) for ref in (ka_ref, kb_ref)]
        values = [ref[:, which].reshape(span, PAIR) for ref in (va_ref, vb_ref)]
        if group == NPR:
            keys.append(kc_ref[...])
            values.append(vc_ref[...])
        probs = [jnp.exp(st - lse) for st in scores_of(keys, q2, bias_ref, group, span)]
        grads = [dot(v, do2, NT) for v in values]
        delta = sum_of([p * g for p, g in zip(probs, grads)])
        ds = [(p * (g - delta)).astype(BF) for p, g in zip(probs, grads)]
        dq = added([dot(k, d, TN) for k, d in zip(keys, ds)])
        dq_ref[rows, :] = (join_heads(dq) * SCALE).astype(BF)
        for i in range(2):
            dk = dot(ds[i], q2).reshape(chips, PR_DEV, PAIR)
            dv = dot(probs[i].astype(BF), do2).reshape(chips, PR_DEV, PAIR)
            at = slice(i * chips, (i + 1) * chips)
            if group < NPR:
                dk_acc[at, group] = dk
                dv_acc[at, group] = dv
            else:
                dk_acc[at, chosen] += dk
                dv_acc[at, chosen] += dv
        if group == NPR:
            dkc_ref[...] = dot(ds[2], q2).astype(BF)
            dvc_ref[...] = dot(probs[2].astype(BF), do2).astype(BF)
    dka_ref[...] = dk_acc[:chips].astype(BF)
    dkb_ref[...] = dk_acc[chips:].astype(BF)
    dva_ref[...] = dv_acc[:chips].astype(BF)
    dvb_ref[...] = dv_acc[chips:].astype(BF)


def attention_specs(chips, rows, first=0):
    q_spec = pl.BlockSpec((rows, PAIR), lambda h, info: (0, first + h))
    k_spec = pl.BlockSpec((chips, NPR, PR_DEV, PAIR), lambda h, info: (0, 0, 0, first + h))
    c_spec = pl.BlockSpec((CLEN, PAIR), lambda h, info: (0, first + h))
    l_spec = pl.BlockSpec((1, 3, TWO), lambda h, info: (first + h, 0, 0))
    return q_spec, k_spec, c_spec, l_spec


def drop_refs(kernel, n_in, n_dep):
    def body(info, *refs):
        kernel(info, *refs[:n_in], *refs[n_in + n_dep :])

    return body


def attention_forward(info, q, keys, values, kc, vc, deps=()):
    k = keys[0]
    chips, rows, pairs = k.shape[0], q.shape[0], q.shape[1] // PAIR
    q_spec, k_spec, c_spec, l_spec = attention_specs(chips, rows)
    return pl.pallas_call(
        drop_refs(attention_forward_kernel, 7, len(deps)),
        grid_spec=pltpu.PrefetchScalarGridSpec(
            num_scalar_prefetch=1,
            grid=(pairs,),
            in_specs=[q_spec] + [k_spec] * 4 + [c_spec, c_spec]
            + [pl.BlockSpec(memory_space=pl.ANY)] * len(deps),
            out_specs=[q_spec, l_spec],
            scratch_shapes=[pltpu.VMEM((2 * chips * PR_DEV, PR_DEV), F32)],
        ),
        out_shape=[shape_of(q.shape, BF), shape_of((pairs, 3, TWO), F32)],
        compiler_params=pltpu.CompilerParams(vmem_limit_bytes=56 * MIB),
        cost_estimate=cost("attention_forward"),
        name="attention_forward",
    )(info, q, *keys, *values, kc, vc, *deps)


def attention_backward(info, q, keys, values, kc, vc, do, lse, first, pairs, before=(), deps=()):
    k = keys[0]
    chips, rows = k.shape[0], q.shape[0]
    q_spec, k_spec, c_spec, l_spec = attention_specs(chips, rows, first)
    deps = list(before) + list(deps)
    return pl.pallas_call(
        drop_refs(attention_backward_kernel, 9, len(deps)),
        grid_spec=pltpu.PrefetchScalarGridSpec(
            num_scalar_prefetch=1,
            grid=(pairs,),
            in_specs=[q_spec] + [k_spec] * 4 + [c_spec, c_spec, q_spec, l_spec]
            + [pl.BlockSpec(memory_space=pl.ANY)] * len(deps),
            out_specs=[q_spec] + [k_spec] * 4 + [c_spec, c_spec],
            scratch_shapes=[
                pltpu.VMEM((2 * chips * PR_DEV, PR_DEV), F32),
                pltpu.VMEM((2 * chips, NPR, PR_DEV, PAIR), F32),
                pltpu.VMEM((2 * chips, NPR, PR_DEV, PAIR), F32),
            ],
        ),
        out_shape=[shape_of(q.shape, BF)]
        + [shape_of(k.shape, BF)] * 4
        + [shape_of(kc.shape, BF)] * 2,
        input_output_aliases={10 + i: i for i in range(len(before))},
        compiler_params=pltpu.CompilerParams(vmem_limit_bytes=60 * MIB),
        cost_estimate=cost("attention_backward"),
        name="attention_backward",
    )(info, q, *keys, *values, kc, vc, do, lse, *deps)


def swap(value, axis, mask):
    size = lax.axis_size(axis)
    return lax.ppermute(value, axis, [(i, i ^ mask) for i in range(size)])


def far_groups(own, dp):
    return [swap(own, "dp", m) for m in range(2, dp, 2)]


def with_neighbours(far):
    return [tokens for even in far for tokens in (even, swap(even, "dp", 1))]


def exchange(blocks):
    return lax.all_to_all(blocks, "expert", split_axis=0, concat_axis=0, tiled=True)


def root(values):
    return lax.rsqrt(jnp.mean(values * values, axis=-1, keepdims=True) + 1e-06)


def norm_back(norm, scale, grad):
    return scale * (grad - norm * jnp.mean(grad * norm, axis=-1, keepdims=True))


def source_row(row):
    inner = jnp.bitwise_and(row, PR_DEV - 1) * NPR + lax.shift_right_logical(row, 7)
    return jnp.where(row < NPR * PR_DEV, inner, row)


def order_matrix(n):
    return (source_row(iota((n, n), 0)) == iota((n, n), 1)).astype(BF)


def order_matrix_t(n):
    return (source_row(iota((n, n), 1)) == iota((n, n), 0)).astype(BF)


def norm_kernel(info, ins, outs, scratch):
    x, gain = ins
    prompt, hidden_ref, ordered = outs
    tokens = dot(order_matrix(x.shape[0]), x[...])
    hidden = (tokens * root(tokens) * gain[...]).astype(BF)
    prompt[...] = hidden[: NPR * PR_DEV]
    hidden_ref[...] = hidden
    ordered[...] = tokens.astype(BF)


def target(rows, k):
    return (rows[HIGH + k : HIGH + k + 1] * 16.0 + rows[LOW + k : LOW + k + 1]).astype(jnp.int32)


def picks_of(rows, slots):
    at = iota((slots, rows.shape[1]), 0)
    return [at == target(rows, k) for k in range(TOP)]


def low(mask):
    return jnp.where(mask, 1.0, 0.0).astype(BF)


def other_routes(rows, picks):
    low_rows = rows[:8].astype(BF)
    first = dot(low_rows, low(picks[0]), NT)[ROUTE + 1 : ROUTE + 2]
    return first + dot(low_rows, low(picks[1]), NT)[ROUTE : ROUTE + 1]


def send_slots(out, sent, per, at=0):
    for m in range(out.shape[0]):
        out[m, at : at + per, :] = sent[m * per : (m + 1) * per]


def clear_others(out):
    for m in range(out.shape[0]):
        out[m, out.shape[1] - TABLE :, :] = jnp.zeros((TABLE, out.shape[2]), BF)


def send_others(out, others, per, at=0):
    row = out.shape[1] - TABLE
    for m in range(out.shape[0]):
        out[m, row:, at : at + per] = jnp.broadcast_to(
            others[:, m * per : (m + 1) * per], (TABLE, per)
        ).astype(BF)


def table_kernel(per, room, capacity):
    def kernel(info, ins, outs, scratch):
        cot, route, slot = ins
        message, cols, out = outs
        n, width = cot.shape
        order = order_matrix(n)
        ordered = dot(order, cot[...]).astype(BF)
        r, s = route[...], slot[...]
        where = jnp.where(s < capacity, r * room + s, -16)
        high = lax.shift_right_arithmetic(where, 4).astype(F32)
        rest = jnp.bitwise_and(where, 15).astype(F32)
        r = r.astype(F32)
        lane = iota((n, 128), 1)
        table = jnp.zeros((n, 128), F32)
        for first, values in ((HIGH, high), (LOW, rest), (ROUTE, r)):
            for k in range(TOP):
                table = jnp.where(lane == first + k, values[:, k : k + 1], table)
        table = dot(order, table.astype(BF))
        cols[...] = table
        rows = table.T[:TABLE]
        message[:n, :] = ordered
        message[n:, :] = jnp.zeros((TABLE, width), BF)
        message[n:, :n] = rows.astype(BF)
        picks = picks_of(rows, per * out.shape[0])
        send_slots(out, dot(low(jnp.logical_or(*picks)), ordered).astype(BF), per)
        clear_others(out)
        send_others(out, other_routes(rows, picks), per)

    return kernel


def table_rows(message):
    n = message.shape[0] - TABLE
    return message[n:, :n].astype(F32)


def dispatch_cot_kernel(per):
    def kernel(info, ins, outs, scratch):
        out, = outs
        n = ins[0].shape[0] - TABLE
        clear_others(out)
        for g, message in enumerate(ins):
            rows = table_rows(message)
            picks = picks_of(rows, per * out.shape[0])
            sent = dot(low(jnp.logical_or(*picks)), message[:n, :]).astype(BF)
            send_slots(out, sent, per, g * per)
            send_others(out, other_routes(rows, picks), per, g * per)

    return kernel


def dispatch_kernel(per):
    def kernel(info, ins, outs, scratch):
        out, = outs
        groups = len(ins) // 2
        for g in range(groups):
            picks = picks_of(table_rows(ins[g]), per * out.shape[0])
            sent = dot(low(jnp.logical_or(*picks)), ins[groups + g][...]).astype(BF)
            send_slots(out, sent, per, g * per)

    return kernel


def middle_kernel(per):
    def kernel(info, ins, outs, scratch):
        ordered, attended, w_out_proj, gain, w_router, cols, message = ins
        middle_ref, second_ref, gates_ref, out = outs
        middle = ordered[...].astype(F32) + dot(attended[...], w_out_proj[...])
        middle_ref[...] = middle
        second = (middle * root(middle) * gain[...]).astype(BF)
        second_ref[...] = second
        picks = picks_of(table_rows(message), per * out.shape[0])
        send_slots(out, dot(low(jnp.logical_or(*picks)), second).astype(BF), per)
        logits = dot(second, w_router[...])
        column = iota(logits.shape, 1).astype(F32)
        chosen = [
            jnp.sum(
                jnp.where(column == cols[:, ROUTE + k : ROUTE + k + 1], logits, 0.0),
                axis=1,
                keepdims=True,
            )
            for k in range(TOP)
        ]
        lane = iota(gates_ref.shape, 1)
        first = 1.0 / (1.0 + jnp.exp(chosen[1] - chosen[0]))
        then = 1.0 / (1.0 + jnp.exp(chosen[0] - chosen[1]))
        gates_ref[...] = jnp.where(lane == 0, first, then)

    return kernel


def combine_kernel():
    def kernel(info, ins, outs, scratch):
        middle_ref, second_ref, gates, cols, message, attended, w_out_proj, w_router, gain = ins[:9]
        came, came_grad = ins[9:]
        out_ref, grad_middle_ref, grad_attended_ref, grad_proj_ref, few_ref = outs
        n, width = middle_ref.shape
        slots = came.shape[0] * came.shape[1]
        middle, second = middle_ref[...], second_ref[...]
        cot = message[:n, :].astype(F32)
        table = cols[...]
        at = iota((n, slots), 1)
        picks = []
        for k in range(TOP):
            where = table[:, HIGH + k : HIGH + k + 1] * 16.0 + table[:, LOW + k : LOW + k + 1]
            picks.append(at == where.astype(jnp.int32))
        returned = came[...].reshape(slots, width)
        fetched = [dot(low(pick), returned) for pick in picks]
        gate = [gates[:, k : k + 1] for k in range(TOP)]
        outputs = (middle + (gate[0] * fetched[0] + gate[1] * fetched[1])).astype(BF)
        out_ref[...] = dot(order_matrix_t(n), outputs).astype(BF)
        grad_gate = [jnp.sum(cot * f, axis=1, keepdims=True) for f in fetched]
        mean_gate = gate[0] * grad_gate[0] + gate[1] * grad_gate[1]
        experts = w_router.shape[1]
        column = iota((n, experts), 1).astype(F32)
        grad_logits = jnp.zeros((n, experts), F32)
        for k in range(TOP):
            grad_logits = jnp.where(
                column == table[:, ROUTE + k : ROUTE + k + 1],
                gate[k] * (grad_gate[k] - mean_gate),
                grad_logits,
            )
        grad_logits = grad_logits.astype(BF)
        grad_second = dot(
            low(jnp.logical_or(*picks)), came_grad[...].reshape(slots, width)
        ) + dot(
            grad_logits, w_router[...], NT
        )
        scale = root(middle)
        norm = middle * scale
        few_ref[:experts, :] = dot(grad_logits, second, TN).astype(BF)
        few_ref[experts:, :] = jnp.broadcast_to(
            jnp.sum(grad_second * norm, axis=0, keepdims=True), (16, width)
        ).astype(BF)
        grad_middle = cot + norm_back(norm, scale, grad_second * gain[...])
        grad_middle_ref[...] = grad_middle
        grad_attn = grad_middle.astype(BF)
        grad_attended_ref[...] = dot(grad_attn, w_out_proj[...], NT).astype(BF)
        grad_proj_ref[...] = dot(attended[...], grad_attn, TN).astype(BF)

    return kernel


def input_kernel(info, ins, outs, scratch):
    grad_q, grad_kc, grad_vc, w_query, w_key, w_value, ordered, gain, grad_middle = ins[:9]
    parts = ins[9:]
    out, = outs
    shares = parts[0][...].astype(F32)
    for part in parts[1:]:
        shares = shares + part[...].astype(F32)
    grad_hidden = dot(grad_q[...], w_query[...], NT) + jnp.concatenate(
        [shares, dot(grad_kc[...], w_key[...], NT) + dot(grad_vc[...], w_value[...], NT)], axis=0
    )
    tokens = ordered[...].astype(F32)
    scale = root(tokens)
    grad = grad_middle[...] + norm_back(tokens * scale, scale, grad_hidden * gain[...])
    back = order_matrix_t(grad.shape[0])
    high = grad.astype(BF)
    rest = grad - high.astype(F32)
    mid = rest.astype(BF)
    last = (rest - mid.astype(F32)).astype(BF)
    out[...] = (dot(back, high) + dot(back, mid)) + dot(back, last)


def halves_kernel(info, ins, outs, scratch):
    kept, came = ins
    for m, out in enumerate(outs):
        out[...] = (kept[m].astype(F32) + came[m].astype(F32)).astype(BF)


def gelu_parts(a):
    square = a * a
    t = jnp.tanh(a * (0.7978845608 + (0.7978845608 * 0.044715) * square))
    half = 0.5 * a
    value = half + half * t
    slope = (0.5 + 0.5 * t) + half * (1.0 - t * t) * (
        0.7978845608 + (0.7978845608 * 3.0 * 0.044715) * square
    )
    return value, slope


def gather_rows(into, blocks, first, room):
    for m in range(blocks.shape[0]):
        into[m * room : (m + 1) * room, :] = blocks[m, pl.ds(pl.multiple_of(first, 16), room), :]


def other_column(others, blocks, first, room):
    at = blocks.shape[1] - TABLE
    span = min(blocks.shape[2], -(-at // 128) * 128)
    eye = iota((room, span), 1) == iota((room, span), 0) + first
    for m in range(blocks.shape[0]):
        row = blocks[m, at : at + TABLE, :span][:1].astype(F32)
        column = jnp.sum(jnp.where(eye, row, 0.0), axis=1, keepdims=True)
        others[m * room : (m + 1) * room, :] = jnp.broadcast_to(column, (room, 128))


def gated(rows, cots, others, w_router, mine):
    logits = dot(rows, w_router)
    column = iota(logits.shape, 1)
    own = jnp.sum(jnp.where(column == mine, logits, 0.0), axis=1, keepdims=True)
    other = others[:, : logits.shape[1]].astype(jnp.int32)
    theirs = jnp.sum(jnp.where(column == other, logits, 0.0), axis=1, keepdims=True)
    gate = 1.0 / (1.0 + jnp.exp(theirs - own))
    return (gate * cots.astype(F32)).astype(BF)


def expert_forward(x_slots, w_in, w_out, room, deps=()):
    devices, per, _ = x_slots.shape
    local, width, units = w_in.shape
    rows = devices * room
    chunk = min(units, 768)
    steps = units // chunk

    def kernel(x_ref, w_in_ref, w_out_ref, *refs):
        slope_ref, out, x, total = refs[len(deps) :]
        l, f = pl.program_id(0), pl.program_id(1)

        @pl.when(f == 0)
        def _():
            gather_rows(x, x_ref, l * room, room)
            total[...] = jnp.zeros_like(total)

        value, slope = gelu_parts(dot(x[...], w_in_ref[0]))
        slope_ref[0] = slope.astype(BF)
        total[...] += dot(value.astype(BF), w_out_ref[0])

        @pl.when(f == steps - 1)
        def _():
            for m in range(devices):
                out[m, pl.ds(pl.multiple_of(l * room, 16), room), :] = total[
                    m * room : (m + 1) * room, :
                ].astype(BF)

    slots = pl.BlockSpec(x_slots.shape, lambda l, f: (0, 0, 0))
    return pl.pallas_call(
        kernel,
        grid=(local, steps),
        in_specs=[
            slots,
            pl.BlockSpec((1, width, chunk), lambda l, f: (l, 0, f)),
            pl.BlockSpec((1, chunk, width), lambda l, f: (l, f, 0)),
        ]
        + [pl.BlockSpec(memory_space=pl.ANY)] * len(deps),
        out_specs=[pl.BlockSpec((1, rows, chunk), lambda l, f: (l, 0, f)), slots],
        out_shape=[shape_of((local, rows, units), BF), shape_of(x_slots.shape, BF)],
        scratch_shapes=[pltpu.VMEM((rows, width), BF), pltpu.VMEM((rows, width), F32)],
        compiler_params=pltpu.CompilerParams(vmem_limit_bytes=56 * MIB),
        cost_estimate=cost("expert_forward"),
        name="expert_forward",
    )(x_slots, w_in, w_out, *deps)


def expert_backward(info, x_slots, c_slots, slope, w_router, w_in, w_out, room, deps=()):
    devices, per, _ = x_slots.shape
    local, width, units = w_in.shape
    rows = devices * room
    chunk = min(units, 768)
    steps = units // chunk

    def kernel(info_ref, x_ref, c_ref, router_ref, slope_ref, w_in_ref, w_out_ref, *refs):
        out, x, grad, others, total = refs[len(deps) :]
        l, f = pl.program_id(0), pl.program_id(1)

        @pl.when(f == 0)
        def _():
            gather_rows(x, x_ref, l * room, room)
            gather_rows(grad, c_ref, l * room, room)
            other_column(others, c_ref, l * room, room)
            grad[...] = gated(
                x[...], grad[...], others[...], router_ref[...], info_ref[0] * local + l
            )
            total[...] = jnp.zeros_like(total)

        grad_act = dot(grad[...], w_out_ref[0], NT)
        grad_pre = (grad_act * slope_ref[0].astype(F32)).astype(BF)
        total[...] += dot(grad_pre, w_in_ref[0], NT)

        @pl.when(f == steps - 1)
        def _():
            for m in range(devices):
                out[m, pl.ds(pl.multiple_of(l * room, 16), room), :] = total[
                    m * room : (m + 1) * room, :
                ].astype(BF)

    slots = pl.BlockSpec(x_slots.shape, lambda l, f, info: (0, 0, 0))
    return pl.pallas_call(
        kernel,
        grid_spec=pltpu.PrefetchScalarGridSpec(
            num_scalar_prefetch=1,
            grid=(local, steps),
            in_specs=[
                slots,
                pl.BlockSpec(c_slots.shape, lambda l, f, info: (0, 0, 0)),
                pl.BlockSpec(w_router.shape, lambda l, f, info: (0, 0)),
                pl.BlockSpec((1, rows, chunk), lambda l, f, info: (l, 0, f)),
                pl.BlockSpec((1, width, chunk), lambda l, f, info: (l, 0, f)),
                pl.BlockSpec((1, chunk, width), lambda l, f, info: (l, f, 0)),
            ]
            + [pl.BlockSpec(memory_space=pl.ANY)] * len(deps),
            out_specs=slots,
            scratch_shapes=[
                pltpu.VMEM((rows, width), BF),
                pltpu.VMEM((rows, width), BF),
                pltpu.VMEM((rows, 128), F32),
                pltpu.VMEM((rows, width), F32),
            ],
        ),
        out_shape=shape_of(x_slots.shape, BF),
        compiler_params=pltpu.CompilerParams(vmem_limit_bytes=56 * MIB),
        cost_estimate=cost("expert_backward"),
        name="expert_backward",
    )(info, x_slots, c_slots, w_router, slope, w_in, w_out, *deps)


def expert_weights(info, groups, w_router, w_in, w_out, room, dp, before=None, last=False, deps=()):
    devices = groups[0][0].shape[0]
    local, width, units = w_in.shape
    part, share = units // dp, width // dp
    per = local * room
    rows = devices * room
    flat = [array for pair in groups for array in pair]
    places = [
        (2 * i, base) for i, (x, _) in enumerate(groups) for base in range(0, x.shape[1], per)
    ]
    n_flat = len(flat)
    sums = [] if before is None else list(before)

    def kernel(info_ref, *refs):
        slots = refs[:n_flat]
        router_ref, w_in_ref, w_out_ref = refs[n_flat : n_flat + 3]
        refs = refs[n_flat + 3 :]
        earlier = refs[: len(sums)]
        refs = refs[len(sums) + len(deps) :]
        out_ref, in_refs = refs[0], refs[1:-4]
        x, grad, others, total = refs[-4:]
        l = pl.program_id(0)
        for g, (place, base) in enumerate(places):
            gather_rows(x, slots[place], base + l * room, room)
            gather_rows(grad, slots[place + 1], base + l * room, room)
            other_column(others, slots[place + 1], base + l * room, room)
            grad[...] = gated(
                x[...], grad[...], others[...], router_ref[...], info_ref[0] * local + l
            )
            value, slope = gelu_parts(dot(x[...], w_in_ref[0]))
            grad_act = dot(grad[...], w_out_ref[0], NT)
            grad_pre = (grad_act * slope).astype(BF)
            part_in = dot(x[...], grad_pre, TN)
            part_out = dot(value.astype(BF), grad[...], TN)
            if g > 0:
                total[...] += part_in
                out_ref[0] += part_out
            elif earlier:
                total[...] = earlier[1][0] + part_in
                out_ref[0] = earlier[0][0] + part_out
            else:
                total[...] = part_in
                out_ref[0] = part_out
        if last:
            for k in range(dp):
                in_refs[0][k, 0] = total[k * share : (k + 1) * share, :].astype(BF)
        else:
            in_refs[0][0] = total[...]

    def const(shape):
        return pl.BlockSpec(shape, lambda l, info: (0,) * len(shape), pipeline_mode=pl.Buffered(1))

    square = pl.BlockSpec((1, part, width), lambda l, info: (l, 0, 0))
    square_in = pl.BlockSpec((1, width, part), lambda l, info: (l, 0, 0))
    if last:
        in_specs = [pl.BlockSpec((dp, 1, share, part), lambda l, info: (0, l, 0, 0))]
        in_shapes = [shape_of((dp, local, share, part), BF)]
    else:
        in_specs = [square_in]
        in_shapes = [shape_of((local, width, part), F32)]
    got = pl.pallas_call(
        kernel,
        grid_spec=pltpu.PrefetchScalarGridSpec(
            num_scalar_prefetch=1,
            grid=(local,),
            in_specs=[const(x.shape) for x in flat]
            + [
                const(w_router.shape),
                pl.BlockSpec((1, width, part), lambda l, info: (l, 0, info[2])),
                pl.BlockSpec((1, part, width), lambda l, info: (l, info[2], 0)),
            ]
            + [square, square_in][: len(sums)]
            + [pl.BlockSpec(memory_space=pl.ANY)] * len(deps),
            out_specs=[square] + in_specs,
            scratch_shapes=[
                pltpu.VMEM((rows, width), BF),
                pltpu.VMEM((rows, width), BF),
                pltpu.VMEM((rows, 128), F32),
                pltpu.VMEM((width, part), F32),
            ],
        ),
        out_shape=[shape_of((local, part, width), F32)] + in_shapes,
        compiler_params=pltpu.CompilerParams(vmem_limit_bytes=60 * MIB),
        cost_estimate=cost("expert_weights_last" if last else "expert_weights"),
        name="expert_weights_last" if last else "expert_weights",
    )(info, *flat, w_router, w_in, w_out, *sums, *deps)
    return got[0], got[1:]


def columns_kernel(info, ins, outs, scratch):
    out, = outs
    pieces, = ins
    part = pieces.shape[3]
    for k in range(pieces.shape[0]):
        out[:, :, k * part : (k + 1) * part] = pieces[k].astype(F32)


class Sums:
    def __init__(self, info, mats, few, dp, devices):
        self.info, self.n, self.dp, self.devices = info, len(mats), dp, devices
        self.rows, self.width = mats[0].shape
        self.chips = devices // 2
        self.half, self.tall = self.width // 2, self.rows // self.chips
        self.short = self.tall // dp
        self.extra = few.shape[0] if few is not None else 0
        self.value = jnp.concatenate(list(mats) + ([few] if self.extra else []), axis=0)
        core = lax.rem(lax.axis_index("expert"), 2)
        self.came = swap(
            lax.dynamic_slice_in_dim(self.value, (1 - core) * self.half, self.half, 1), "expert", 1
        )

    @staticmethod
    def fits(rows, width, dp, devices):
        short = rows // (devices // 2) // dp
        return short % 16 == 0 and width % 256 == 0 and short * dp * (devices // 2) == rows

    def cores(self, deps=()):
        n, rows, tall, half, extra = self.n, self.rows, self.tall, self.half, self.extra

        def kernel(info_ref, ins, outs, scratch):
            kept, got = ins
            lanes = pl.ds(pl.multiple_of(info_ref[3] * half, 128), half)
            for m, out in enumerate(outs):
                for i in range(n):
                    start = i * rows + jnp.bitwise_xor(info_ref[4], m) * tall
                    at = pl.ds(pl.multiple_of(start, 16), tall)
                    out[i * tall : (i + 1) * tall, :] = (
                        kept[at, lanes].astype(F32) + got[at, :].astype(F32)
                    ).astype(BF)
                if extra:
                    out[n * tall :, :] = (
                        kept[n * rows :, lanes].astype(F32) + got[n * rows :, :].astype(F32)
                    ).astype(BF)

        pieces = run(
            kernel, "sum_cores", self.info, [self.value, self.came],
            [shape_of((n * tall + extra, half), BF)] * self.chips, deps=deps,
        )
        self.pieces = [pieces[0]] + [
            swap(pieces[m], "expert", 2 * m) for m in range(1, self.chips)
        ]
        return pieces[0]

    def planes(self, deps=()):
        n, tall, short, half, extra = self.n, self.tall, self.short, self.half, self.extra

        def kernel(info_ref, ins, outs, scratch):
            total, = scratch
            total[...] = added([piece[...].astype(F32) for piece in ins]).astype(BF)
            for k, out in enumerate(outs):
                for i in range(n):
                    start = i * tall + jnp.bitwise_xor(info_ref[2], k) * short
                    out[i * short : (i + 1) * short, :] = total[
                        pl.ds(pl.multiple_of(start, 16), short), :
                    ]
                if extra:
                    out[n * short :, :] = total[n * tall :, :]

        pieces = run(
            kernel, "sum_chips", self.info, self.pieces,
            [shape_of((n * short + extra, half), BF)] * self.dp,
            scratch=[pltpu.VMEM((n * tall + extra, half), BF)], deps=deps,
        )
        self.pieces = [pieces[0]] + [swap(pieces[k], "dp", k) for k in range(1, self.dp)]
        return pieces[0]

    def groups(self, deps=()):
        n, short, half, extra = self.n, self.short, self.half, self.extra

        def kernel(info_ref, ins, outs, scratch):
            value = added([piece[...].astype(F32) for piece in ins]).astype(BF)
            outs[0][...] = value[: n * short]
            if extra:
                outs[1][...] = value[n * short :]

        got = run(
            kernel, "sum_groups", self.info, self.pieces,
            [shape_of((n * short, half), BF)] + ([shape_of((extra, half), BF)] if extra else []),
            deps=deps,
        )
        self.few = list(got[1:])
        self.own = [got[0]] + [swap(got[0], "dp", k) for k in range(1, self.dp)]
        return got[0]

    def gather(self):
        spread = jnp.concatenate(self.own, axis=0)
        self.spread = jnp.concatenate(
            [spread] + [swap(spread, "expert", 2 * m) for m in range(1, self.chips)] + self.few, axis=0
        )
        self.other = swap(self.spread, "expert", 1)

    def finish(self, columns, gain, weights, deps=()):
        n, short, tall, half, extra = self.n, self.short, self.tall, self.half, self.extra
        chips, dp, rows = self.chips, self.dp, self.rows

        def kernel(info_ref, ins, outs, scratch):
            for c, ref in enumerate(ins[:2]):
                lanes = pl.ds(pl.multiple_of(jnp.bitwise_xor(info_ref[3], c) * half, 128), half)
                for m in range(chips):
                    for k in range(dp):
                        start = jnp.bitwise_xor(info_ref[4], m) * tall
                        start = start + jnp.bitwise_xor(info_ref[2], k) * short
                        at = pl.ds(pl.multiple_of(start, 16), short)
                        for i in range(n):
                            place = ((m * dp + k) * n + i) * short
                            outs[i][at, lanes] = ref[place : place + short, :].astype(F32)
                scratch[0][:, lanes] = ref[chips * dp * n * short :, :].astype(F32)
            outs[n][...] = scratch[0][:columns, :].T
            outs[n + 1][...] = scratch[0][columns : columns + 1, :]
            outs[n + 2][...] = gained(zip(ins[3:], outs), ins[2][...])

        row = shape_of((1, self.width), F32)
        return run(
            kernel, "spread_sums", self.info, [self.spread, self.other, gain] + list(weights),
            [shape_of((rows, self.width), F32)] * n + [shape_of((self.width, columns), F32), row, row],
            scratch=[pltpu.VMEM((extra, self.width), F32)], deps=deps,
        )


def gained(pairs, gain):
    total = 0.0
    for weight, grad in pairs:
        total = total + jnp.sum(weight[...].astype(F32) * grad[...], axis=1, keepdims=True)
    return jnp.broadcast_to(total, (total.shape[0], 128)).T[:1] / gain


def per_device(
    inputs,
    gain_one,
    w_query,
    w_key,
    w_value,
    w_out_proj,
    gain_two,
    w_router,
    w_in,
    w_out,
    routes,
    slot_index,
    prompt_of,
    cotangent,
):
    row_count, width = inputs.shape[1], inputs.shape[2]
    dp, devices = lax.axis_size("dp"), lax.axis_size("expert")
    z, device = lax.axis_index("dp"), lax.axis_index("expert")
    chips = devices // 2
    prompt_rows = NPR * PR_DEV
    expert_count, local = w_router.shape[1], w_in.shape[0]
    capacity = max(2, 5 * row_count * TOP // (4 * expert_count))
    room = -(-capacity // 16) * 16
    per = local * room
    info = jnp.stack(
        [device, prompt_of[0, 0], z, lax.rem(device, 2), lax.div(device, 2)]
    ).astype(jnp.int32)
    gain_one = gain_one[None, :]
    gain_two = gain_two[None, :]
    wide = shape_of((row_count, width), BF)
    wide32 = shape_of((row_count, width), F32)
    narrow = shape_of((row_count, 128), F32)
    x_shape = shape_of((devices, per, width), BF)
    c_shape = shape_of((devices, per + TABLE, width), BF)

    hidden_p, hidden, ordered = run(
        norm_kernel, "norm", info, [inputs[0], gain_one],
        [shape_of((prompt_rows, width), BF), wide, wide],
    )
    near = [hidden_p] + [swap(hidden_p, "expert", 2 * m) for m in range(1, chips)]

    message, cols, c_sent = run(
        table_kernel(per, room, capacity), "table", info,
        [cotangent[0], routes[0], slot_index[0]],
        [shape_of((row_count + TABLE, width), BF), narrow, c_shape],
        deps=[hidden_p],
    )
    near, message = lax.optimization_barrier((near, message))
    near = jnp.concatenate(near, axis=0)
    far = swap(near, "expert", 1)
    messages = far_groups(message, dp)
    c_sent, near = lax.optimization_barrier((c_sent, near))
    c_slots = [exchange(c_sent)]

    queries = dot(hidden, w_query).astype(BF)
    hidden_c = hidden[prompt_rows:]
    key_c = dot(hidden_c, w_key).astype(BF)
    value_c = dot(hidden_c, w_value).astype(BF)

    def heads(rows, weight):
        return dot(rows, weight).astype(BF).reshape(chips, NPR, PR_DEV, width)

    keys = [heads(near, w_key), heads(far, w_key)]
    values = [heads(near, w_value), heads(far, w_value)]
    attended, lse = attention_forward(info, queries, keys, values, key_c, value_c)
    c_slots, messages, attended = lax.optimization_barrier((c_slots, messages, attended))
    messages = with_neighbours(messages)
    c_odd = [swap(c_slots[0], "dp", 1)]

    middle, second, gates, x_sent = run(
        middle_kernel(per), "middle", info,
        [ordered, attended, w_out_proj, gain_two, w_router, cols, message],
        [wide32, wide, narrow, x_shape],
    )
    x_slots = [exchange(x_sent)]
    seconds = far_groups(second, dp)
    c_rest = run(
        dispatch_cot_kernel(per), "dispatch_cot", info, messages,
        [shape_of((devices, (dp - 2) * per + TABLE, width), BF)], deps=[middle],
    )
    x_slots, c_rest = lax.optimization_barrier((x_slots, c_rest))
    c_slots = c_slots + [exchange(sent) for sent in c_rest]
    x_odd = [swap(x_slots[0], "dp", 1)]

    slope, out_sent = expert_forward(x_slots[0], w_in, w_out, room)
    seconds, slope = lax.optimization_barrier((seconds, slope))
    seconds = with_neighbours(seconds)
    returned = exchange(out_sent)
    grad_sent = expert_backward(
        info, x_slots[0], c_slots[0], slope, w_router, w_in, w_out, room, deps=c_slots[1:]
    )
    returned, grad_sent = lax.optimization_barrier((returned, grad_sent))
    grad_returned = exchange(grad_sent)

    sums = expert_weights(
        info, [(x_slots[0], c_slots[0])], w_router, w_in, w_out, room, dp,
        deps=[grad_sent],
    )
    x_rest = run(
        dispatch_kernel(per), "dispatch", info, messages + seconds,
        [shape_of((devices, (dp - 2) * per, width), BF)], deps=[sums[0]],
    )

    outputs, grad_middle, grad_attended, grad_proj, few = run(
        combine_kernel(), "combine", info,
        [middle, second, gates, cols, message, attended, w_out_proj, w_router, gain_two]
        + [returned, grad_returned],
        [wide, wide32, wide, shape_of((width, width), BF), shape_of((expert_count + 16, width), BF)],
        deps=x_rest,
    )
    x_slots = x_slots + [exchange(sent) for sent in x_rest]

    pairs = width // PAIR

    def back(first, count, before=(), deps=()):
        return attention_backward(
            info, queries, keys, values, key_c, value_c, grad_attended, lse, first, count,
            before=before, deps=deps,
        )

    got = back(0, pairs, deps=c_odd + x_odd)
    grad_q, dk_near, dk_far, dv_near, dv_far, grad_kc, grad_vc = got
    grad_q, dk_near, dk_far, dv_near, dv_far, x_slots[1] = lax.optimization_barrier(
        (grad_q, dk_near, dk_far, dv_near, dv_far, x_slots[1])
    )
    dk_near, dk_far, dv_near, dv_far = [
        part.reshape(chips * prompt_rows, width) for part in (dk_near, dk_far, dv_near, dv_far)
    ]
    grad_query = dot(hidden, grad_q, TN).astype(BF)
    grad_key = (dot(near, dk_near, TN) + dot(far, dk_far, TN) + dot(hidden_c, grad_kc, TN)).astype(BF)
    grad_value = (dot(near, dv_near, TN) + dot(far, dv_far, TN) + dot(hidden_c, grad_vc, TN)).astype(BF)
    dense = [grad_query, grad_key, grad_value, grad_proj]
    stepwise = Sums.fits(width, width, dp, devices)
    if stepwise:
        total = Sums(info, dense, few, dp, devices)

    sent = (dot(dk_far, w_key, NT) + dot(dv_far, w_value, NT)).astype(BF)
    kept = (dot(dk_near, w_key, NT) + dot(dv_near, w_value, NT)).astype(BF)
    came = swap(sent.reshape(chips, prompt_rows, width), "expert", 1)
    after = total.cores([kept]) if stepwise else kept
    shares = run(
        halves_kernel, "halves", info, [kept.reshape(chips, prompt_rows, width), came],
        [shape_of((prompt_rows, width), BF)] * chips, deps=[after],
    )

    grad_w_out, in_pieces = expert_weights(
        info, [(x_odd[0], c_odd[0]), (x_slots[1], c_slots[1])], w_router, w_in, w_out, room, dp,
        before=(sums[0], sums[1][0]), last=True, deps=[shares[0]],
    )
    shares, in_pieces, grad_w_out = lax.optimization_barrier((shares, in_pieces, grad_w_out))
    shares = [shares[0]] + [swap(shares[m], "expert", 2 * m) for m in range(1, chips)]
    after = [grad_w_out]
    if stepwise:
        after = [total.planes(after)]
        after = [total.groups(after + shares)]
        total.own[0], in_pieces = lax.optimization_barrier((total.own[0], in_pieces))
    grad_input, = run(
        input_kernel, "input", info,
        [grad_q, grad_kc, grad_vc, w_query, w_key, w_value, ordered, gain_one, grad_middle] + shares,
        [wide32], deps=after,
    )
    if stepwise:
        total.own, grad_input = lax.optimization_barrier((total.own, grad_input))
        total.gather()
    in_pieces = lax.all_to_all(in_pieces[0], "dp", split_axis=0, concat_axis=0, tiled=True)
    after = []
    if stepwise:
        query_sum, key_sum, value_sum, proj_sum, grad_router, grad_gain_two, grad_gain_one = (
            total.finish(expert_count, gain_one, [w_query, w_key, w_value])
        )
        after = [query_sum]
    else:
        query_sum, key_sum, value_sum, proj_sum, few = lax.psum(
            [part.astype(F32) for part in dense + [few]], ("dp", "expert")
        )
        grad_router, grad_gain_two = few[:expert_count].T, few[expert_count :][:1]
        grad_gain_one = gained(
            [(w_query, query_sum), (w_key, key_sum), (w_value, value_sum)], gain_one
        )
    grad_w_in, = run(
        columns_kernel, "columns", info, [in_pieces],
        [shape_of((local, width // dp, w_in.shape[2]), F32)], deps=after,
    )
    return (
        outputs[None],
        grad_input[None],
        grad_gain_one[0],
        query_sum,
        key_sum,
        value_sum,
        proj_sum,
        grad_gain_two[0],
        grad_router,
        grad_w_in,
        grad_w_out,
    )


def solution(mesh):
    return jax.shard_map(
        per_device,
        mesh=mesh,
        in_specs=(
            P("dp", "expert", None),
            P(),
            P(),
            P(),
            P(),
            P(),
            P(),
            P(),
            P("expert", None, None),
            P("expert", None, None),
            P("dp", "expert", None),
            P("dp", "expert", None),
            P("dp", "expert"),
            P("dp", "expert", None),
        ),
        out_specs=(
            P("dp", "expert", None),
            P("dp", "expert", None),
            P(),
            P(),
            P(),
            P(),
            P(),
            P(),
            P(),
            P("expert", "dp", None),
            P("expert", "dp", None),
        ),
        check_vma=False,
    )
```

time: 756 us -> 442 us (0.58)
  waiting for transfers between devices: 286 us -> 114 us
  Pallas kernels: 39 us -> 183 us
  matrix products: 172 us -> 40.2 us
  blocking collectives: 47.3 us -> 0 us
  local copies, waits for them, and re-layouts: 72.7 us -> 31.1 us
  starting transfers between devices: 97.7 us -> 65 us
  other arithmetic: 28.5 us -> 2.56 us
    pallas_call x2 -> x19, Pallas kernels: 39 us -> 183 us  [the longest x13 66.3 us: run(): pl.pallas_call(body, in_specs=[pl.BlockSpec(memory_space=pltpu.SMEM)] + [...]
    ppermute x42 -> x28, waiting for transfers between devices: 234 us -> 95 us  [swap(): return lax.ppermute(value, axis, [(i, i ^ mask) for i in range(size)])]
    dot_general x52 -> x18, matrix products: 172 us -> 40.2 us  [dot(): return lax.dot_general(a, b, (dims, ((), ())), preferred_element_type=F32)]
    all_to_all x2 -> x0, blocking collectives: 47.3 us -> none  [to_experts(): lax.all_to_all(slots, 'expert', split_axis=0, concat_axis=0, tiled=True)]
    all_to_all x10 -> x7, waiting for transfers between devices: 51.5 us -> 18.7 us  [the longest x1 11.1 us: per_device(): lax.all_to_all(in_pieces[0], 'dp', split_axis=0, concat_axis=0, tiled=True)]
    slice x16 -> x0, local copies, waits for them, and re-layouts: 22.7 us -> none  [the longest x4 9.05 us: weighted(): rows_in[l]]
    ppermute x42 -> x28, starting transfers between devices: 54.2 us -> 34.3 us  [swap(): return lax.ppermute(value, axis, [(i, i ^ mask) for i in range(size)])]
    unnamed x196 -> x94, local copies, waits for them, and re-layouts: 9.85 us -> 26.3 us
  transfers between devices with their start and end apart: 52 -> 35, of which waited for: 27 -> 16; matrix products, arithmetic and copies ran while one was open for 26% -> 9% of each run, Pallas kernels for 0% -> 39%
where the time goes in v2:
time: 442 us; the launch traced here: 437 us
  Pallas kernels  183 us (41%)
  waiting for transfers between devices  114 us (26%)
  starting transfers between devices  65 us (15%)
  matrix products  40.2 us (9%)
  local copies, waits for them, and re-layouts  31.1 us (7%)
    ppermute x28, waiting for transfers between devices, swap(): return lax.ppermute(value, axis, [(i, i ^ mask) for i in range(size)])  95 us
    pallas_call x13, Pallas kernels, run(): pl.pallas_call(body, in_specs=[pl.BlockSpec(memory_space=pltpu.SMEM)] + [...  66.3 us
    dot_general x18, matrix products, dot(): return lax.dot_general(a, b, (dims, ((), ())), preferred_element_type=F32)  40.2 us
    pallas_call x2, Pallas kernels, expert_weights(): pl.pallas_call(kernel, grid_spec=pltpu.PrefetchScalarGridSpec(num_scalar_...  38.6 us
    ppermute x28, starting transfers between devices, swap(): return lax.ppermute(value, axis, [(i, i ^ mask) for i in range(size)])  34.3 us
    all_to_all x6, starting transfers between devices, exchange(): lax.all_to_all(blocks, 'expert', split_axis=0, concat_axis=0, tiled=True)  27 us
    unnamed x94, local copies, waits for them, and re-layouts  26.3 us
    pallas_call x1, Pallas kernels, attention_backward(): pl.pallas_call(drop_refs(attention_backward_kernel, 9, len(deps)), grid_s...  22.2 us
  transfers between devices with their start and end apart: 35, of which 16 were waited for; matrix products, arithmetic and copies ran while one was open for 9% of the time, Pallas kernels for 39%

profile of v2, /device:TPU:0, one launch (start us, length us, event | category | flops | bytes accessed | tf_op | source)
XLA Modules:
  0.0 437.2 jit_solution(7606353782743084517)
XLA Ops:
  12.1 4.5 %table.1 = (bf16[400,768]{1,0:T(8,128)(2,1)}, f32[384,128]{1,0:T(8,128)}, bf16[8,144,768]{2,1,0:T(8,128)(2,1)}) custom-call(s32[5]{0:T(128)} %stack.19.info_ref.info, bf16[384,768]{1,0:T(8,128)(2,1)} %bitcast.59, s32[384,2]{1,0:T(8,128)} %bitcast.55, s32[384,2]{1,0:T(8,128)} %bitcast.56, bf16[256,768]{1,0:T(8,128)(2,1)} %get-tuple-element.101.refs_3_), custom_call_target="tpu_custom_call" | custom-call | flops 4950000128 | tf_op jit(solution)/shard_map/table/pallas_call | solution.py:81
  20.1 7.6 %collective-permute-done.1 = bf16[256,768]{1,0:T(8,128)(2,1)S(1)} collective-permute-done((bf16[256,768]{1,0:T(8,128)(2,1)}, bf16[256,768]{1,0:T(8,128)(2,1)S(1)}, u32[]{:S(2)}, u32[]{:S(2)}) %collective-permute-start.1) | collective-permute-done | bytes 393248 | tf_op jit(solution)/shard_map/ppermute | solution.py:295
  40.3 4.5 %all-to-all-start = ((bf16[8,144,768]{2,1,0:T(8,128)(2,1)}), bf16[8,144,768]{2,1,0:T(8,128)(2,1)}, u32[]{:S(2)}, u32[]{:S(2)}) async-start(bf16[8,144,768]{2,1,0:T(8,128)(2,1)} %get-tuple-element.105), calls=%async_computation | async-start | bytes 3538944 | tf_op jit(solution)/shard_map/all_to_all | solution.py:307
  44.7 4.0 convolution_convert_fusion.1
  60.6 15.3 %attention_forward.1 = (bf16[384,768]{1,0:T(8,128)(2,1)}, f32[6,3,256]{2,1,0:T(4,128)}) custom-call(s32[5]{0:T(128)} %stack.19.info_ref.info, bf16[384,768]{1,0:T(8,128)(2,1)} %convolution_convert_fusion.5.refs_0_, bf16[4,2,128,768]{3,2,1,0:T(8,128)(2,1)} %bitcast.62, bf16[4,2,128,768]{3,2,1,0:T(8,128)(2,1)} %bitcast.66, bf16[4,2,128,768]{3,2,1,0:T(8,128)(2,1)} %bitcast.60, ...), custom_call_target="tpu_custom_call" | custom-call | flops 16499999744 | tf_op jit(solution)/shard_map/attention_forward/pallas_call | solution.py:247
  75.9 5.2 %middle.1 = (f32[384,768]{1,0:T(8,128)}, bf16[384,768]{1,0:T(8,128)(2,1)}, f32[384,128]{1,0:T(8,128)}, bf16[8,128,768]{2,1,0:T(8,128)(2,1)}) custom-call(s32[5]{0:T(128)} %stack.19.info_ref.info, bf16[384,768]{1,0:T(8,128)(2,1)} %get-tuple-element.97.refs_0_.refs_6_, bf16[384,768]{1,0:T(8,128)(2,1)} %get-tuple-element.110.refs_1_.refs_5_, ...), custom_call_target="tpu_custom_call" | custom-call | flops 5609999872 | tf_op jit(solution)/shard_map/middle/pallas_call | solution.py:81
  81.1 4.3 all-to-all-start.1
  87.0 14.8 %collective-permute-done.5.refs_1_ = bf16[400,768]{1,0:T(8,128)(2,1)S(1)} collective-permute-done((bf16[400,768]{1,0:T(8,128)(2,1)}, bf16[400,768]{1,0:T(8,128)(2,1)S(1)}, u32[]{:S(2)}, u32[]{:S(2)}) %collective-permute-start.5) | collective-permute-done | bytes 614432 | tf_op jit(solution)/shard_map/ppermute | solution.py:295
  102.6 5.6 %dispatch_cot.1 = bf16[8,272,768]{2,1,0:T(8,128)(2,1)} custom-call(s32[5]{0:T(128)} %stack.19.info_ref.info, bf16[400,768]{1,0:T(8,128)(2,1)} %collective-permute-done.3.refs_0_, bf16[400,768]{1,0:T(8,128)(2,1)} %copy-done.24, f32[384,768]{1,0:T(8,128)} %get-tuple-element.112.refs_2_.refs_0_), custom_call_target="tpu_custom_call" | custom-call | flops 7699999744 | tf_op jit(solution)/shard_map/dispatch_cot/pallas_call | solution.py:81
  108.3 4.8 %all-to-all-start.3 = ((bf16[8,272,768]{2,1,0:T(8,128)(2,1)}), bf16[8,272,768]{2,1,0:T(8,128)(2,1)}, u32[]{:S(2)}, u32[]{:S(2)}) async-start(bf16[8,272,768]{2,1,0:T(8,128)(2,1)} %dispatch_cot.1), calls=%async_computation.3 | async-start | bytes 6684672 | tf_op jit(solution)/shard_map/all_to_all | solution.py:307
  115.4 20.4 %expert_forward.1 = (bf16[2,512,3072]{2,1,0:T(8,128)(2,1)}, bf16[8,128,768]{2,1,0:T(8,128)(2,1)}) custom-call(bf16[8,128,768]{2,1,0:T(8,128)(2,1)} %all-to-all-done.1.x_ref.refs_0_, bf16[2,768,3072]{2,1,0:T(8,128)(2,1)} %refs_5_.3, bf16[2,3072,768]{2,1,0:T(8,128)(2,1)} %refs_6_.3), custom_call_target="tpu_custom_call" | custom-call | flops 22000001024 | tf_op jit(solution)/shard_map/expert_forward/pallas_call | solution.py:612
  135.7 30.8 %collective-permute-done.6.refs_2_ = bf16[384,768]{1,0:T(8,128)(2,1)} collective-permute-done((bf16[384,768]{1,0:T(8,128)(2,1)S(1)}, bf16[384,768]{1,0:T(8,128)(2,1)}, u32[]{:S(2)}, u32[]{:S(2)}) %collective-permute-start.6) | collective-permute-done | bytes 589856 | tf_op jit(solution)/shard_map/ppermute | solution.py:295
  167.7 4.3 all-to-all-start.2
  172.0 20.0 %expert_backward.1.refs_5_ = bf16[8,128,768]{2,1,0:T(8,128)(2,1)} custom-call(s32[5]{0:T(128)} %stack.19.info_ref.info, bf16[8,128,768]{2,1,0:T(8,128)(2,1)} %all-to-all-done.1.x_ref.refs_0_, bf16[8,144,768]{2,1,0:T(8,128)(2,1)} %all-to-all-done.c_ref.refs_1_, bf16[768,16]{1,0:T(8,128)(2,1)} %copy.27.refs_4_.router_ref.refs_2_.refs_7_, ...), custom_call_target="tpu_custom_call" | custom-call | flops 22000001024 | tf_op jit(solution)/shard_map/expert_backward/pallas_call | solution.py:663
  193.0 4.3 all-to-all-start.4
  197.3 11.4 %expert_weights.1 = (f32[2,768,768]{2,1,0:T(8,128)}, f32[2,768,768]{2,1,0:T(8,128)}) custom-call(s32[5]{0:T(128)} %stack.19.info_ref.info, bf16[8,128,768]{2,1,0:T(8,128)(2,1)} %all-to-all-done.1.x_ref.refs_0_, bf16[8,144,768]{2,1,0:T(8,128)(2,1)} %all-to-all-done.c_ref.refs_1_, bf16[768,16]{1,0:T(8,128)(2,1)} %copy.27.refs_4_.router_ref.refs_2_.refs_7_, ...), custom_call_target="tpu_custom_call" | custom-call | flops 9900000256 | tf_op jit(solution)/shard_map/expert_weights/pallas_call | solution.py:752
  208.8 4.6 %collective-permute-done.7.refs_3_ = bf16[384,768]{1,0:T(8,128)(2,1)S(1)} collective-permute-done((bf16[384,768]{1,0:T(8,128)(2,1)}, bf16[384,768]{1,0:T(8,128)(2,1)S(1)}, u32[]{:S(2)}, u32[]{:S(2)}) %collective-permute-start.7) | collective-permute-done | bytes 589856 | tf_op jit(solution)/shard_map/ppermute | solution.py:295
  214.1 5.1 %dispatch.1.refs_11_ = bf16[8,256,768]{2,1,0:T(8,128)(2,1)} custom-call(s32[5]{0:T(128)} %stack.19.info_ref.info, bf16[400,768]{1,0:T(8,128)(2,1)} %collective-permute-done.3.refs_0_, bf16[400,768]{1,0:T(8,128)(2,1)} %copy-done.24, bf16[384,768]{1,0:T(8,128)(2,1)} %collective-permute-done.6.refs_2_, bf16[384,768]{1,0:T(8,128)(2,1)} %copy-done.29, ...), custom_call_target="tpu_custom_call" | custom-call | flops 7150000128 | tf_op jit(solution)/shard_map/dispatch/pallas_call | solution.py:81
  219.2 4.8 %all-to-all-start.5 = ((bf16[8,256,768]{2,1,0:T(8,128)(2,1)}), bf16[8,256,768]{2,1,0:T(8,128)(2,1)}, u32[]{:S(2)}, u32[]{:S(2)}) async-start(bf16[8,256,768]{2,1,0:T(8,128)(2,1)} %dispatch.1.refs_11_), calls=%async_computation.5 | async-start | bytes 6291456 | tf_op jit(solution)/shard_map/all_to_all | solution.py:307
  224.1 9.2 %combine.1 = (bf16[384,768]{1,0:T(8,128)(2,1)}, f32[384,768]{1,0:T(8,128)}, bf16[384,768]{1,0:T(8,128)(2,1)}, bf16[768,768]{1,0:T(8,128)(2,1)}, bf16[32,768]{1,0:T(8,128)(2,1)}) custom-call(s32[5]{0:T(128)} %stack.19.info_ref.info, f32[384,768]{1,0:T(8,128)} %get-tuple-element.112.refs_2_.refs_0_, bf16[384,768]{1,0:T(8,128)(2,1)} %get-tuple-element.113.refs_1_, ...), custom_call_target="tpu_custom_call" | custom-call | flops 10560000000 | tf_op jit(solution)/shard_map/combine/pallas_call | solution.py:81
  233.3 22.2 %attention_backward.1 = (bf16[384,768]{1,0:T(8,128)(2,1)}, bf16[4,2,128,768]{3,2,1,0:T(8,128)(2,1)}, bf16[4,2,128,768]{3,2,1,0:T(8,128)(2,1)}, bf16[4,2,128,768]...) custom-call(s32[5]{0:T(128)} %stack.19.info_ref.info, ...), custom_call_target="tpu_custom_call" | custom-call | flops 16499999744 | tf_op jit(solution)/shard_map/attention_backward/pallas_call | solution.py:269
  255.5 6.4 %all-to-all-done.5.refs_2_ = bf16[8,256,768]{2,1,0:T(8,128)(2,1)} async-done(((bf16[8,256,768]{2,1,0:T(8,128)(2,1)}), bf16[8,256,768]{2,1,0:T(8,128)(2,1)}, u32[]{:S(2)}, u32[]{:S(2)}) %all-to-all-start.5) | async-done | bytes 3145760 | tf_op jit(solution)/shard_map/all_to_all | solution.py:307
  288.2 5.1 %sum_cores.1 = (bf16[800,384]{1,0:T(8,128)(2,1)}, bf16[800,384]{1,0:T(8,128)(2,1)}, bf16[800,384]{1,0:T(8,128)(2,1)}, bf16[800,384]{1,0:T(8,128)(2,1)}) custom-call(s32[5]{0:T(128)} %stack.19.info_ref.info, bf16[3104,768]{1,0:T(8,128)(2,1)} %copy-done.3, bf16[3104,384]{1,0:T(8,128)(2,1)} %collective-permute-done.10.refs_1_, ...), custom_call_target="tpu_custom_call" | custom-call | flops 4400000000 | tf_op jit(solution)/shard_map/sum_cores/pallas_call | solution.py:81
  301.1 27.2 %expert_weights_last.1 = (f32[2,768,768]{2,1,0:T(8,128)}, bf16[4,2,192,768]{3,2,1,0:T(8,128)(2,1)}) custom-call(s32[5]{0:T(128)} %stack.19.info_ref.info, bf16[8,128,768]{2,1,0:T(8,128)(2,1)} %collective-permute-done.9.refs_10_.refs_0_, bf16[8,144,768]{2,1,0:T(8,128)(2,1)} %collective-permute-done.8.refs_9_.refs_1_, ...), custom_call_target="tpu_custom_call" | custom-call | flops 32999999488 | tf_op jit(solution)/shard_map/expert_weights_last/pallas_call | solution.py:752
  347.3 5.4 %collective-permute-done.16.refs_2_ = bf16[224,384]{1,0:T(8,128)(2,1)S(1)} collective-permute-done((bf16[224,384]{1,0:T(8,128)(2,1)}, bf16[224,384]{1,0:T(8,128)(2,1)S(1)}, u32[]{:S(2)}, u32[]{:S(2)}) %collective-permute-start.16) | collective-permute-done | bytes 172064 | tf_op jit(solution)/shard_map/ppermute | solution.py:295
  359.7 8.3 %input.1 = f32[384,768]{1,0:T(8,128)} custom-call(s32[5]{0:T(128)} %stack.19.info_ref.info, bf16[384,768]{1,0:T(8,128)(2,1)} %get-tuple-element.135.refs_0_, bf16[128,768]{1,0:T(8,128)(2,1)} %get-tuple-element.138.refs_1_, bf16[128,768]{1,0:T(8,128)(2,1)} %get-tuple-element.141.refs_2_, bf16[768,768]{1,0:T(8,128)(2,1)} %refs_3_.5, bf16[768,768]{1,0:T(8,128)(2,1)} %refs_4_.7, ...), custom_call_target="tpu_custom_call" | custom-call | flops 1100000000 | tf_op jit(solution)/shard_map/input/pallas_call | solution.py:81
  379.7 9.5 %collective-permute-done.24 = bf16[768,384]{1,0:T(8,128)(2,1)} collective-permute-done((bf16[768,384]{1,0:T(8,128)(2,1)}, bf16[768,384]{1,0:T(8,128)(2,1)}, u32[]{:S(2)}, u32[]{:S(2)}) %collective-permute-start.24) | collective-permute-done | bytes 589856 | tf_op jit(solution)/shard_map/ppermute | solution.py:295
  391.1 8.0 %collective-permute-done.25 = bf16[768,384]{1,0:T(8,128)(2,1)S(1)} collective-permute-done((bf16[768,384]{1,0:T(8,128)(2,1)}, bf16[768,384]{1,0:T(8,128)(2,1)S(1)}, u32[]{:S(2)}, u32[]{:S(2)}) %collective-permute-start.25) | collective-permute-done | bytes 589856 | tf_op jit(solution)/shard_map/ppermute | solution.py:295
  401.5 4.8 %collective-permute-done.27.refs_1_ = bf16[3104,384]{1,0:T(8,128)(2,1)S(1)} collective-permute-done((bf16[3104,384]{1,0:T(8,128)(2,1)}, bf16[3104,384]{1,0:T(8,128)(2,1)S(1)}, u32[]{:S(2)}, u32[]{:S(2)}) %collective-permute-start.27) | collective-permute-done | bytes 2383904 | tf_op jit(solution)/shard_map/ppermute | solution.py:295
  407.7 8.2 %spread_sums.1 = (f32[768,768]{1,0:T(8,128)}, f32[768,768]{1,0:T(8,128)}, f32[768,768]{1,0:T(8,128)}, f32[768,768]{1,0:T(8,128)}, f32[768,16]{1,0:T(8,128)}, /*index=5*/f32[1,768]{1,0:T(1,128)}, f32[1,768]{1,0:T(1,128)}) custom-call(s32[5]{0:T(128)} %stack.19.info_ref.info, bf16[3104,384]{1,0:T(8,128)(2,1)} %constant_dynamic-update-slice_fusion.10.refs_0_, ...), custom_call_target="tpu_custom_call" | custom-call | flops 9900000256 | tf_op jit(solution)/shard_map/spread_sums/pallas_call | solution.py:81
  420.2 11.1 %all-to-all-done.6.refs_0_ = bf16[4,2,192,768]{3,2,1,0:T(8,128)(2,1)S(1)} async-done(((bf16[4,2,192,768]{3,2,1,0:T(8,128)(2,1)}), bf16[4,2,192,768]{3,2,1,0:T(8,128)(2,1)S(1)}, u32[]{:S(2)}, u32[]{:S(2)}) %all-to-all-start.6) | async-done | bytes 2359328 | tf_op jit(solution)/shard_map/all_to_all | solution.py:1083
  432.7 4.2 columns.1
  (179 shorter events, 129.4 us)
Async XLA Ops:
  6.0 14.1 %collective-permute-start.2 = (bf16[256,768]{1,0:T(8,128)(2,1)}, bf16[256,768]{1,0:T(8,128)(2,1)S(1)}, u32[]{:S(2)}, u32[]{:S(2)}) collective-permute-start(bf16[256,768]{1,0:T(8,128)(2,1)} %get-tuple-element.101.refs_3_), channel_id=1, source_target_pairs={{0,6},{1,7},{2,4},{3,5},{4,2},{5,3},{6,0},{7,1},{8,14},{9,15},{10,... | collective-permute-start | bytes 1179656 | tf_op jit(solution)/shard_map/ppermute | solution.py:295
  9.9 17.7 %collective-permute-start.1 = (bf16[256,768]{1,0:T(8,128)(2,1)}, bf16[256,768]{1,0:T(8,128)(2,1)S(1)}, u32[]{:S(2)}, u32[]{:S(2)}) collective-permute-start(bf16[256,768]{1,0:T(8,128)(2,1)} %get-tuple-element.101.refs_3_), channel_id=1, source_target_pairs={{0,4},{1,5},{2,6},{3,7},{4,0},{5,1},{6,2},{7,3},{8,12},{9,13},{10,... | collective-permute-start | bytes 1179656 | tf_op jit(solution)/shard_map/ppermute | solution.py:295
  10.4 17.5 %collective-permute-start = (bf16[256,768]{1,0:T(8,128)(2,1)}, bf16[256,768]{1,0:T(8,128)(2,1)S(1)}, u32[]{:S(2)}, u32[]{:S(2)}) collective-permute-start(bf16[256,768]{1,0:T(8,128)(2,1)} %get-tuple-element.101.refs_3_), channel_id=1, source_target_pairs={{0,2},{1,3},{2,0},{3,1},{4,6},{5,7},{6,4},{7,5},{8,10},{9,11},{10,... | collective-permute-start | bytes 1179656 | tf_op jit(solution)/shard_map/ppermute | solution.py:295
  32.6 20.2 %collective-permute-start.4 = (bf16[1024,768]{1,0:T(8,128)(2,1)}, bf16[1024,768]{1,0:T(8,128)(2,1)}, u32[]{:S(2)}, u32[]{:S(2)}) collective-permute-start(bf16[1024,768]{1,0:T(8,128)(2,1)} %constant_dynamic-update-slice_fusion), channel_id=1, source_target_pairs={{0,1},{1,0},{2,3},{3,2},{4,5},{5,4},{6,7},{7,6},{8,9},{9,8},{10,11... | collective-permute-start | bytes 4718600 | tf_op jit(solution)/shard_map/ppermute | solution.py:295
  37.5 38.4 %collective-permute-start.3 = (bf16[400,768]{1,0:T(8,128)(2,1)}, bf16[400,768]{1,0:T(8,128)(2,1)}, u32[]{:S(2)}, u32[]{:S(2)}) collective-permute-start(bf16[400,768]{1,0:T(8,128)(2,1)} %get-tuple-element.106.refs_6_.refs_4_), channel_id=1, source_target_pairs={{0,16},{8,24},{16,0},{24,8},{1,17},{9,25},{17,1},{25,9},{2,18},{10... | collective-permute-start | bytes 1843208 | tf_op jit(solution)/shard_map/ppermute | solution.py:295
  40.3 35.6 %all-to-all-start = ((bf16[8,144,768]{2,1,0:T(8,128)(2,1)}), bf16[8,144,768]{2,1,0:T(8,128)(2,1)}, u32[]{:S(2)}, u32[]{:S(2)}) async-start(bf16[8,144,768]{2,1,0:T(8,128)(2,1)} %get-tuple-element.105), calls=%async_computation | async-start | bytes 3538944 | tf_op jit(solution)/shard_map/all_to_all | solution.py:307
  81.1 27.2 %all-to-all-start.1 = ((bf16[8,128,768]{2,1,0:T(8,128)(2,1)}), bf16[8,128,768]{2,1,0:T(8,128)(2,1)}, u32[]{:S(2)}, u32[]{:S(2)}) async-start(bf16[8,128,768]{2,1,0:T(8,128)(2,1)} %get-tuple-element.115), calls=%async_computation.1 | async-start | bytes 3145728 | tf_op jit(solution)/shard_map/all_to_all | solution.py:307
  85.4 16.5 %collective-permute-start.5 = (bf16[400,768]{1,0:T(8,128)(2,1)}, bf16[400,768]{1,0:T(8,128)(2,1)S(1)}, u32[]{:S(2)}, u32[]{:S(2)}) collective-permute-start(bf16[400,768]{1,0:T(8,128)(2,1)} %collective-permute-done.3.refs_0_), channel_id=1, source_target_pairs={{0,8},{8,0},{16,24},{24,16},{1,9},{9,1},{17,25},{25,17},{2,10},{10... | collective-permute-start | bytes 1843208 | tf_op jit(solution)/shard_map/ppermute | solution.py:295
  108.3 59.4 %all-to-all-start.3 = ((bf16[8,272,768]{2,1,0:T(8,128)(2,1)}), bf16[8,272,768]{2,1,0:T(8,128)(2,1)}, u32[]{:S(2)}, u32[]{:S(2)}) async-start(bf16[8,272,768]{2,1,0:T(8,128)(2,1)} %dispatch_cot.1), calls=%async_computation.3 | async-start | bytes 6684672 | tf_op jit(solution)/shard_map/all_to_all | solution.py:307
  113.1 120.2 %collective-permute-start.8 = (bf16[8,144,768]{2,1,0:T(8,128)(2,1)}, bf16[8,144,768]{2,1,0:T(8,128)(2,1)}, u32[]{:S(2)}, u32[]{:S(2)}) collective-permute-start(bf16[8,144,768]{2,1,0:T(8,128)(2,1)} %all-to-all-done.c_ref.refs_1_), channel_id=1, source_target_pairs={{0,8},{8,0},{16,24},{24,16},{1,9},{9,1},{17,25},{25,17},{2,10},{10... | collective-permute-start | bytes 5308424 | tf_op jit(solution)/shard_map/ppermute | solution.py:295
  114.7 51.8 %collective-permute-start.6 = (bf16[384,768]{1,0:T(8,128)(2,1)S(1)}, bf16[384,768]{1,0:T(8,128)(2,1)}, u32[]{:S(2)}, u32[]{:S(2)}) collective-permute-start(bf16[384,768]{1,0:T(8,128)(2,1)S(1)} %copy-done.28), channel_id=1, source_target_pairs={{0,16},{8,24},{16,0},{24,8},{1,17},{9,25},{17,1},{25,9},{2,18},{10... | collective-permute-start | bytes 1769480 | tf_op jit(solution)/shard_map/ppermute | solution.py:295
  115.1 118.2 %collective-permute-start.9 = (bf16[8,128,768]{2,1,0:T(8,128)(2,1)}, bf16[8,128,768]{2,1,0:T(8,128)(2,1)}, u32[]{:S(2)}, u32[]{:S(2)}) collective-permute-start(bf16[8,128,768]{2,1,0:T(8,128)(2,1)} %all-to-all-done.1.x_ref.refs_0_), channel_id=1, source_target_pairs={{0,8},{8,0},{16,24},{24,16},{1,9},{9,1},{17,25},{25,17},{2,10},{10... | collective-permute-start | bytes 4718600 | tf_op jit(solution)/shard_map/ppermute | solution.py:295
  166.5 46.8 %collective-permute-start.7 = (bf16[384,768]{1,0:T(8,128)(2,1)}, bf16[384,768]{1,0:T(8,128)(2,1)S(1)}, u32[]{:S(2)}, u32[]{:S(2)}) collective-permute-start(bf16[384,768]{1,0:T(8,128)(2,1)} %collective-permute-done.6.refs_2_), channel_id=1, source_target_pairs={{0,8},{8,0},{16,24},{24,16},{1,9},{9,1},{17,25},{25,17},{2,10},{10... | collective-permute-start | bytes 1769480 | tf_op jit(solution)/shard_map/ppermute | solution.py:295
  167.7 25.3 %all-to-all-start.2 = ((bf16[8,128,768]{2,1,0:T(8,128)(2,1)}), bf16[8,128,768]{2,1,0:T(8,128)(2,1)}, u32[]{:S(2)}, u32[]{:S(2)}) async-start(bf16[8,128,768]{2,1,0:T(8,128)(2,1)} %get-tuple-element.118), calls=%async_computation.2 | async-start | bytes 3145728 | tf_op jit(solution)/shard_map/all_to_all | solution.py:307
  193.0 26.2 %all-to-all-start.4 = ((bf16[8,128,768]{2,1,0:T(8,128)(2,1)}), bf16[8,128,768]{2,1,0:T(8,128)(2,1)}, u32[]{:S(2)}, u32[]{:S(2)}) async-start(bf16[8,128,768]{2,1,0:T(8,128)(2,1)} %expert_backward.1.refs_5_), calls=%async_computation.4 | async-start | bytes 3145728 | tf_op jit(solution)/shard_map/all_to_all | solution.py:307
  219.2 42.8 %all-to-all-start.5 = ((bf16[8,256,768]{2,1,0:T(8,128)(2,1)}), bf16[8,256,768]{2,1,0:T(8,128)(2,1)}, u32[]{:S(2)}, u32[]{:S(2)}) async-start(bf16[8,256,768]{2,1,0:T(8,128)(2,1)} %dispatch.1.refs_11_), calls=%async_computation.5 | async-start | bytes 6291456 | tf_op jit(solution)/shard_map/all_to_all | solution.py:307
  283.6 13.2 %collective-permute-start.14 = (bf16[4,256,768]{2,1,0:T(8,128)(2,1)S(1)}, bf16[4,256,768]{2,1,0:T(8,128)(2,1)S(1)}, u32[]{:S(2)}, u32[]{:S(2)}) collective-permute-start(bf16[4,256,768]{2,1,0:T(8,128)(2,1)S(1)} %bitcast.57), channel_id=1, source_target_pairs={{0,1},{1,0},{2,3},{3,2},{4,5},{5,4},{6,7},{7,6},{8,9},{9,8},{10,11... | collective-permute-start | bytes 4718600 | tf_op jit(solution)/shard_map/ppermute | solution.py:295
  293.3 36.2 %collective-permute-start.11 = (bf16[800,384]{1,0:T(8,128)(2,1)}, bf16[800,384]{1,0:T(8,128)(2,1)S(1)}, u32[]{:S(2)}, u32[]{:S(2)}) collective-permute-start(bf16[800,384]{1,0:T(8,128)(2,1)} %get-tuple-element.145), channel_id=1, source_target_pairs={{0,2},{1,3},{2,0},{3,1},{4,6},{5,7},{6,4},{7,5},{8,10},{9,11},{10,... | collective-permute-start | bytes 1843208 | tf_op jit(solution)/shard_map/ppermute | solution.py:295
  293.8 38.1 %collective-permute-start.12 = (bf16[800,384]{1,0:T(8,128)(2,1)}, bf16[800,384]{1,0:T(8,128)(2,1)S(1)}, u32[]{:S(2)}, u32[]{:S(2)}) collective-permute-start(bf16[800,384]{1,0:T(8,128)(2,1)} %get-tuple-element.146), channel_id=1, source_target_pairs={{0,4},{1,5},{2,6},{3,7},{4,0},{5,1},{6,2},{7,3},{8,12},{9,13},{10,... | collective-permute-start | bytes 1843208 | tf_op jit(solution)/shard_map/ppermute | solution.py:295
  294.5 37.5 %collective-permute-start.13 = (bf16[800,384]{1,0:T(8,128)(2,1)}, bf16[800,384]{1,0:T(8,128)(2,1)S(1)}, u32[]{:S(2)}, u32[]{:S(2)}) collective-permute-start(bf16[800,384]{1,0:T(8,128)(2,1)} %get-tuple-element.147), channel_id=1, source_target_pairs={{0,6},{1,7},{2,4},{3,5},{4,2},{5,3},{6,0},{7,1},{8,14},{9,15},{10,... | collective-permute-start | bytes 1843208 | tf_op jit(solution)/shard_map/ppermute | solution.py:295
  328.3 12.1 %collective-permute-start.18 = (bf16[256,768]{1,0:T(8,128)(2,1)S(1)}, bf16[256,768]{1,0:T(8,128)(2,1)S(1)}, u32[]{:S(2)}, u32[]{:S(2)}) collective-permute-start(bf16[256,768]{1,0:T(8,128)(2,1)S(1)} %copy-done.32), channel_id=1, source_target_pairs={{0,2},{1,3},{2,0},{3,1},{4,6},{5,7},{6,4},{7,5},{8,10},{9,11},{10,... | collective-permute-start | bytes 1179656 | tf_op jit(solution)/shard_map/ppermute | solution.py:295
  328.9 18.4 %collective-permute-start.19 = (bf16[256,768]{1,0:T(8,128)(2,1)S(1)}, bf16[256,768]{1,0:T(8,128)(2,1)S(1)}, u32[]{:S(2)}, u32[]{:S(2)}) collective-permute-start(bf16[256,768]{1,0:T(8,128)(2,1)S(1)} %copy-done.31), channel_id=1, source_target_pairs={{0,4},{1,5},{2,6},{3,7},{4,0},{5,1},{6,2},{7,3},{8,12},{9,13},{10,... | collective-permute-start | bytes 1179656 | tf_op jit(solution)/shard_map/ppermute | solution.py:295
  329.5 17.8 %collective-permute-start.20 = (bf16[256,768]{1,0:T(8,128)(2,1)S(1)}, bf16[256,768]{1,0:T(8,128)(2,1)S(1)}, u32[]{:S(2)}, u32[]{:S(2)}) collective-permute-start(bf16[256,768]{1,0:T(8,128)(2,1)S(1)} %copy-done.30), channel_id=1, source_target_pairs={{0,6},{1,7},{2,4},{3,5},{4,2},{5,3},{6,0},{7,1},{8,14},{9,15},{10,... | collective-permute-start | bytes 1179656 | tf_op jit(solution)/shard_map/ppermute | solution.py:295
  336.7 10.6 %collective-permute-start.15 = (bf16[224,384]{1,0:T(8,128)(2,1)}, bf16[224,384]{1,0:T(8,128)(2,1)S(1)}, u32[]{:S(2)}, u32[]{:S(2)}) collective-permute-start(bf16[224,384]{1,0:T(8,128)(2,1)} %get-tuple-element.158), channel_id=1, source_target_pairs={{0,8},{8,0},{16,24},{24,16},{1,9},{9,1},{17,25},{25,17},{2,10},{10... | collective-permute-start | bytes 516104 | tf_op jit(solution)/shard_map/ppermute | solution.py:295
  338.2 14.5 %collective-permute-start.16 = (bf16[224,384]{1,0:T(8,128)(2,1)}, bf16[224,384]{1,0:T(8,128)(2,1)S(1)}, u32[]{:S(2)}, u32[]{:S(2)}) collective-permute-start(bf16[224,384]{1,0:T(8,128)(2,1)} %get-tuple-element.159), channel_id=1, source_target_pairs={{0,16},{8,24},{16,0},{24,8},{1,17},{9,25},{17,1},{25,9},{2,18},{10... | collective-permute-start | bytes 516104 | tf_op jit(solution)/shard_map/ppermute | solution.py:295
  340.4 12.3 %collective-permute-start.17 = (bf16[224,384]{1,0:T(8,128)(2,1)}, bf16[224,384]{1,0:T(8,128)(2,1)S(1)}, u32[]{:S(2)}, u32[]{:S(2)}) collective-permute-start(bf16[224,384]{1,0:T(8,128)(2,1)} %get-tuple-element.160), channel_id=1, source_target_pairs={{0,24},{8,16},{16,8},{24,0},{1,25},{9,17},{17,9},{25,1},{2,26},{10... | collective-permute-start | bytes 516104 | tf_op jit(solution)/shard_map/ppermute | solution.py:295
  355.3 12.7 %collective-permute-start.23 = (bf16[192,384]{1,0:T(8,128)(2,1)}, bf16[192,384]{1,0:T(8,128)(2,1)S(1)}, u32[]{:S(2)}, u32[]{:S(2)}) collective-permute-start(bf16[192,384]{1,0:T(8,128)(2,1)} %get-tuple-element.170.refs_13_), channel_id=1, source_target_pairs={{0,24},{8,16},{16,8},{24,0},{1,25},{9,17},{17,9},{25,1},{2,26},{10... | collective-permute-start | bytes 442376 | tf_op jit(solution)/shard_map/ppermute | solution.py:295
  357.0 12.7 %collective-permute-start.22 = (bf16[192,384]{1,0:T(8,128)(2,1)}, bf16[192,384]{1,0:T(8,128)(2,1)S(1)}, u32[]{:S(2)}, u32[]{:S(2)}) collective-permute-start(bf16[192,384]{1,0:T(8,128)(2,1)} %get-tuple-element.170.refs_13_), channel_id=1, source_target_pairs={{0,16},{8,24},{16,0},{24,8},{1,17},{9,25},{17,1},{25,9},{2,18},{10... | collective-permute-start | bytes 442376 | tf_op jit(solution)/shard_map/ppermute | solution.py:295
  372.6 16.6 %collective-permute-start.24 = (bf16[768,384]{1,0:T(8,128)(2,1)}, bf16[768,384]{1,0:T(8,128)(2,1)}, u32[]{:S(2)}, u32[]{:S(2)}) collective-permute-start(bf16[768,384]{1,0:T(8,128)(2,1)} %get-tuple-element.194), channel_id=1, source_target_pairs={{0,2},{1,3},{2,0},{3,1},{4,6},{5,7},{6,4},{7,5},{8,10},{9,11},{10,... | collective-permute-start | bytes 1769480 | tf_op jit(solution)/shard_map/ppermute | solution.py:295
  373.1 26.0 %collective-permute-start.25 = (bf16[768,384]{1,0:T(8,128)(2,1)}, bf16[768,384]{1,0:T(8,128)(2,1)S(1)}, u32[]{:S(2)}, u32[]{:S(2)}) collective-permute-start(bf16[768,384]{1,0:T(8,128)(2,1)} %get-tuple-element.194), channel_id=1, source_target_pairs={{0,4},{1,5},{2,6},{3,7},{4,0},{5,1},{6,2},{7,3},{8,12},{9,13},{10,... | collective-permute-start | bytes 1769480 | tf_op jit(solution)/shard_map/ppermute | solution.py:295
  373.8 26.3 %collective-permute-start.26 = (bf16[768,384]{1,0:T(8,128)(2,1)}, bf16[768,384]{1,0:T(8,128)(2,1)S(1)}, u32[]{:S(2)}, u32[]{:S(2)}) collective-permute-start(bf16[768,384]{1,0:T(8,128)(2,1)} %get-tuple-element.194), channel_id=1, source_target_pairs={{0,6},{1,7},{2,4},{3,5},{4,2},{5,3},{6,0},{7,1},{8,14},{9,15},{10,... | collective-permute-start | bytes 1769480 | tf_op jit(solution)/shard_map/ppermute | solution.py:295
  376.1 55.2 %all-to-all-start.6 = ((bf16[4,2,192,768]{3,2,1,0:T(8,128)(2,1)}), bf16[4,2,192,768]{3,2,1,0:T(8,128)(2,1)S(1)}, u32[]{:S(2)}, u32[]{:S(2)}) async-start(bf16[4,2,192,768]{3,2,1,0:T(8,128)(2,1)} %get-tuple-element.182), calls=%async_computation.6 | async-start | bytes 4718592 | tf_op jit(solution)/shard_map/all_to_all | solution.py:1083
  (43 other events, 255.0 us)
